TPU v7x, 256 devices: a whole 4x4x8 slice. The times are simulated.
256 devices in a mesh: gx: 32 (over y, x, core), gy: 8 (over z).
Axes of the slice: x: 4, y: 4, z: 8, core: 2. Of those that a mesh axis runs over, the one named last changes fastest.
Arguments:
- positions: float32 [3, 8388608], P(None, ('gx', 'gy')), may hold values from -0.5 to 1.5
- charges: float32 [8388608], P(('gx', 'gy')), may hold values from -0.09375 to 0.09375
- moment_freq: float32 [3, 121], replicated, may hold values from -2 to 2
- moment_phase: float32 [121], replicated, may hold values from -3.140625 to 3.140625
- m2l_ops: float32 [16, 121, 121], replicated, may hold values from -0.09375 to 0.09375
- child_parent_shift_matrix: float32 [8, 121, 121], replicated, may hold values from -0.1875 to 0.1875
- send_leaf: int32 [256, 256, 2], P(('gx', 'gy')), may hold values from 0 to 63
- send_count: int32 [256, 256], P(('gx', 'gy')), may hold values from 0 to 2, as said below
- far_src: int32 [16384, 32], P(('gx', 'gy')), may hold values from -1 to 575, as said below
- far_class: int32 [16384, 32], P(('gx', 'gy')), may hold values from 0 to 15
- near_src: int32 [16384, 8], P(('gx', 'gy')), may hold values from -1 to 575, as said below
- near_shift: int32 [16384, 8], P(('gx', 'gy')), may hold values from 0 to 26
- top_list: int32 [256, 32], P(('gx', 'gy')), may hold values from 0 to 255
- top_class: int32 [256, 32], P(('gx', 'gy')), may hold values from 0 to 15
Outputs:
- potential: float32 [8388608], P(('gx', 'gy'))
Inputs may be any that keep to these rules, and one draw needn't show every extreme that they name: send_count[p, d] slots of sender p toward receiver d carry a leaf; the last device fills all 2 slots toward every receiver. `far_src`: an entry of leaf g on device d is -1 (padding), an own leaf i < 64, or 64 + p * 2 + s with s < send_count[p, d]. `near_src`: as for far_src; the first entry of each leaf is the leaf itself.
All inputs are finite; a program needn't handle non-finite values.
Results may differ from a plain program's by a relative error of at most 0.0003.
Values sent between devices are 32-bit elements; how exact they have to be, the bound alone decides.
A program may use at most 128 MiB of HBM per device.

v0:
```python
import math

import jax
import jax.numpy as jnp
from jax import lax
from jax.sharding import PartitionSpec as P

TWO_PI = 2.0 * math.pi
SOFTENING = 0.01
EXACT_PRECISION = lax.Precision.HIGHEST


def features(place, moment_freq, moment_phase):
    phase_arg = (
        moment_freq[0][:, None] * place[0][None, :]
        + moment_freq[1][:, None] * place[1][None, :]
        + moment_freq[2][:, None] * place[2][None, :]
    )
    return jnp.cos(TWO_PI * phase_arg + moment_phase[:, None])


def class_table(classes, number):
    return (classes[..., None] == jnp.arange(number, dtype=jnp.int32)).astype(jnp.float32)


def offset_vector(shift_class_index):
    return (
        (shift_class_index % 3 - 1).astype(jnp.float32),
        (shift_class_index // 3 % 3 - 1).astype(jnp.float32),
        (shift_class_index // 9 - 1).astype(jnp.float32),
    )


def near_block(target_bodies, sources, weights, shift_class_index):
    accumulated = jnp.zeros((target_bodies.shape[0], target_bodies.shape[2]), jnp.float32)
    for column in range(sources.shape[1]):
        source = sources[:, column]
        shift_x, shift_y, shift_z = offset_vector(shift_class_index[:, column])
        delta_x = target_bodies[:, 0, :, None] - (source[:, 0, None, :] + shift_x[:, None, None])
        delta_y = target_bodies[:, 1, :, None] - (source[:, 1, None, :] + shift_y[:, None, None])
        delta_z = target_bodies[:, 2, :, None] - (source[:, 2, None, :] + shift_z[:, None, None])
        radius = delta_x * delta_x + delta_y * delta_y + delta_z * delta_z + SOFTENING
        summed = jnp.sum(source[:, 3, None, :] * lax.rsqrt(radius), axis=2)
        accumulated = accumulated + summed * weights[:, column, None]
    return accumulated


def local(
    positions,
    charges,
    moment_freq,
    moment_phase,
    m2l_ops,
    child_parent_shift_matrix,
    send_leaf,
    send_count,
    far_src,
    far_class,
    near_src,
    near_shift,
    top_list,
    top_class,
):
    coef_count = moment_phase.shape[0]
    leaves = far_src.shape[0]
    leaf_width = charges.shape[0] // leaves
    slot_count = send_leaf.shape[2]
    peer_count = send_leaf.shape[1]
    offsets = m2l_ops.shape[0]
    harmonic = features(positions, moment_freq, moment_phase).reshape(
        coef_count, leaves, leaf_width
    )
    charge_rows = charges.reshape(leaves, leaf_width)
    moments = jnp.einsum("klb,lb->lk", harmonic, charge_rows, precision=EXACT_PRECISION)
    grouped_moments = moments.reshape(leaves // 8, 8, coef_count).sum(axis=0)
    own_top = jnp.einsum(
        "cij,cj->i", child_parent_shift_matrix, grouped_moments, precision=EXACT_PRECISION
    )
    all_tops = lax.all_gather(own_top[None, :], ("gx", "gy"), axis=0, tiled=True)
    picked = all_tops[top_list[0]]
    top_grouped = jnp.einsum(
        "ec,ej->cj", class_table(top_class[0], offsets), picked, precision=EXACT_PRECISION
    )
    root_local_expansion = jnp.einsum("cij,cj->i", m2l_ops, top_grouped, precision=EXACT_PRECISION)
    downward_sweep = jnp.einsum(
        "cji,j->ci", child_parent_shift_matrix, root_local_expansion, precision=EXACT_PRECISION
    )
    leaf_bodies = (
        jnp.concatenate([positions, charges[None, :]], axis=0)
        .reshape(4, leaves, leaf_width)
        .transpose(1, 0, 2)
    )
    slot_live = (jnp.arange(slot_count, dtype=jnp.int32)[None, :] < send_count[0][:, None]).astype(
        jnp.float32
    )
    chosen = send_leaf[0]
    coarse_size = lax.axis_size("gx")
    fine_size = lax.axis_size("gy")
    out_moments = (moments[chosen] * slot_live[:, :, None]).reshape(
        coarse_size, fine_size, slot_count, coef_count
    )
    out_bodies = (leaf_bodies[chosen] * slot_live[:, :, None, None]).reshape(
        coarse_size, fine_size, slot_count, 4, leaf_width
    )
    in_moments, in_bodies = (
        lax.all_to_all(
            lax.all_to_all(out_moments, "gx", split_axis=0, concat_axis=0, tiled=True),
            "gy",
            split_axis=1,
            concat_axis=1,
            tiled=True,
        ),
        lax.all_to_all(
            lax.all_to_all(out_bodies, "gx", split_axis=0, concat_axis=0, tiled=True),
            "gy",
            split_axis=1,
            concat_axis=1,
            tiled=True,
        ),
    )
    pool_moments = jnp.concatenate(
        [moments, in_moments.reshape(peer_count * slot_count, coef_count)], axis=0
    )
    pool_bodies = jnp.concatenate(
        [leaf_bodies, in_bodies.reshape(peer_count * slot_count, 4, leaf_width)], axis=0
    )
    far_usable = (far_src >= 0).astype(jnp.float32)
    vectors = pool_moments[jnp.maximum(far_src, 0)] * far_usable[..., None]
    grouped = jnp.einsum(
        "lec,lej->lcj", class_table(far_class, offsets), vectors, precision=EXACT_PRECISION
    )
    local_exp = jnp.einsum("cij,lcj->li", m2l_ops, grouped, precision=EXACT_PRECISION)
    local_exp = (local_exp.reshape(leaves // 8, 8, coef_count) + downward_sweep[None]).reshape(
        leaves, coef_count
    )
    far_field = jnp.einsum("klb,lk->lb", harmonic, local_exp, precision=EXACT_PRECISION)
    near_usable = (near_src >= 0).astype(jnp.float32)
    near_index = jnp.maximum(near_src, 0)
    near_width = near_src.shape[1]

    def near_step(inputs):
        target_bodies, pointers, weights, shift_class_index = inputs
        return near_block(target_bodies, pool_bodies[pointers], weights, shift_class_index)

    near_field = lax.map(
        near_step,
        (
            leaf_bodies[:, :3].reshape(leaves // 8, 8, 3, leaf_width),
            near_index.reshape(leaves // 8, 8, near_width),
            near_usable.reshape(leaves // 8, 8, near_width),
            near_shift.reshape(leaves // 8, 8, near_width),
        ),
    )
    return near_field.reshape(leaves * leaf_width) + far_field.reshape(leaves * leaf_width)


def solution(mesh):
    placed = (
        P(None, ("gx", "gy")),
        P(("gx", "gy")),
        P(),
        P(),
        P(),
        P(),
        P(("gx", "gy"), None, None),
        P(("gx", "gy"), None),
        P(("gx", "gy"), None),
        P(("gx", "gy"), None),
        P(("gx", "gy"), None),
        P(("gx", "gy"), None),
        P(("gx", "gy"), None),
        P(("gx", "gy"), None),
    )
    return jax.shard_map(
        local, mesh=mesh, in_specs=placed, out_specs=P(("gx", "gy")), check_vma=False
    )
```

profile of v0, /device:TPU:6, one launch (start us, length us, event | category | flops | bytes accessed | tf_op | source)
XLA Modules:
  0.0 821.2 jit_solution(4706428727633397207)
XLA Ops:
  13.2 56.1 %add_cosine_fusion = f32[121,64,512]{2,1,0:T(8,128)S(1)} fusion(f32[121]{0:T(128)} %param.19, f32[64,512]{1,0:T(8,128)S(1)} %mul.613, f32[121]{0:T(128)S(1)} %get-tuple-element.348, f32[64,512]{1,0:T(8,128)S(1)} %mul.608, f32[121]{0:T(128)S(1)} %get-tuple-element.349, f32[64,512]{1,0:T(8,128)S(1)} %mul.603, f32[121]{0:T(128)S(1)} %get-tuple-element.347), kind=kLoop, calls=%fused_computation.241 | loop fusion | flops 27754496 | bytes 16254864 | tf_op jit(solution)/shard_map/cos | solution.py:19
  69.4 23.4 %fusion.58 = f32[64,1,121]{2,1,0:T(1,128)S(1)} fusion(f32[64,512,1]{1,2,0:T(1,128)S(1)} %bitcast.354, f32[121,64,512]{2,1,0:T(8,128)S(1)} %add_cosine_fusion), kind=kOutput, calls=%fused_computation.239 | convolution fusion | flops 47579136 | bytes 16021760 | tf_op jit(solution)/shard_map/klb,lb->lk/dot_general | solution.py:74
  94.9 7.6 all-to-all-start.2
  102.7 4.7 gather_fusion.1
  107.4 4.0 broadcast_multiply_fusion
  111.4 7.4 all-to-all-start
  119.7 48.0 %all-to-all-done = f32[32,8,2,4,512]{4,3,2,1,0:T(4,128)} async-done(((f32[32,8,2,4,512]{4,3,2,1,0:T(4,128)}), f32[32,8,2,4,512]{4,3,2,1,0:T(4,128)}, u32[]{:S(2)}, u32[]{:S(2)}) %all-to-all-start) | async-done | bytes 4194336 | tf_op jit(solution)/shard_map/all_to_all | solution.py:114
  167.7 8.5 %all-to-all-start.3 = ((f32[32,8,2,121]{3,2,0,1:T(2,128)}), f32[32,8,2,121]{3,2,0,1:T(2,128)S(1)}, u32[]{:S(2)}, u32[]{:S(2)}) async-start(f32[32,8,2,121]{3,2,0,1:T(2,128)} %copy.74), calls=%async_computation.3 | async-start | bytes 524288 | tf_op jit(solution)/shard_map/all_to_all | solution.py:106
  176.2 5.6 copy.68
  181.8 5.7 all-to-all-done.3
  187.5 4.5 all-to-all-start.1
  198.4 274.9 %all-reduce.3.cloned.1.call-done = f32[30976]{0:T(1024)} async-done(((f32[30976]{0:T(1024)}), f32[30976]{0:T(1024)}) %all-reduce.3.cloned.1.call-update) | async-done | bytes 123920
  477.1 5.5 gather_fusion.3
  484.2 22.5 %fusion.56 = f32[64,1,512]{2,1,0:T(1,128)S(1)} fusion(f32[64,121,1]{1,2,0:T(1,128)S(1)} %bitcast.391, f32[121,64,512]{2,1,0:T(8,128)} %copy-done.1), kind=kOutput, calls=%fused_computation.237 | convolution fusion | flops 47579136 | bytes 16021760 | tf_op jit(solution)/shard_map/klb,lk->lb/dot_general | solution.py:136
  506.8 3.6 copy.69
  513.6 299.8 %while.13 = (s32[]{:T(128)}, f32[8,8,512]{2,1,0:T(8,128)S(1)}, s32[8,8,8]{2,1,0:T(8,128)S(1)}, f32[576,4,512]{2,1,0:T(4,128)}, f32[8,8,3,512]{3,1,2,0:T(8,128)},...) while((s32[]{:T(128)}, f32[8,8,512]{2,1,0:T(8,128)S(1)}, s32[8,8,8]{2,1,0:T(8,128)S(1)}, ...), condition=%wide.region_9.10_spmd, body=%wide.region_0.9_spmd.sunk | while | flops 184679488 | bytes 5307241 | solution.py:145
  520.3 14.7 %multiply_reduce_fusion.11 = (f32[8,512]{1,0:T(8,128)S(1)}, f32[8,512]{1,0:T(8,128)S(1)}, f32[8,512]{1,0:T(8,128)S(1)}, f32[8,512]{1,0:T(8,128)S(1)}) fusion(f32[8,512]{1,0:T(8,128)S(1)} %bitcast.375, f32[8,512]{1,0:T(8,128)S(1)} %get-tuple-element.538, f32[8,512]{1,0:T(8,128)S(1)} %bitcast.376, f32[8,512]{1,0:T(8,128)S(1)} %get-tuple-element.539, ...), kind=kLoop, calls=%fused_computation.12.clone.1 | loop fusion | flops 92258304 | bytes 376832 | tf_op jit(solution)/shard_map/while/body/eval_jaxpr/reduce_sum | solution.py:43
  535.5 14.7 %multiply_reduce_fusion.10 = (f32[8,512]{1,0:T(8,128)S(1)}, f32[8,512]{1,0:T(8,128)S(1)}, f32[8,512]{1,0:T(8,128)S(1)}, f32[8,512]{1,0:T(8,128)S(1)}) fusion(f32[8,512]{1,0:T(8,128)S(1)} %bitcast.380, f32[8,512]{1,0:T(8,128)S(1)} %bitcast.382, f32[8,512]{1,0:T(8,128)S(1)} %bitcast.384, f32[8,512]{1,0:T(8,128)S(1)} %bitcast.385, ...), kind=kLoop, calls=%fused_computation.8.clone.1 | loop fusion | flops 92258304 | bytes 376832 | tf_op jit(solution)/shard_map/while/body/eval_jaxpr/reduce_sum | solution.py:43
  557.7 14.7 %multiply_reduce_fusion.11 = (f32[8,512]{1,0:T(8,128)S(1)}, f32[8,512]{1,0:T(8,128)S(1)}, f32[8,512]{1,0:T(8,128)S(1)}, f32[8,512]{1,0:T(8,128)S(1)}) fusion(f32[8,512]{1,0:T(8,128)S(1)} %bitcast.375, f32[8,512]{1,0:T(8,128)S(1)} %get-tuple-element.538, f32[8,512]{1,0:T(8,128)S(1)} %bitcast.376, f32[8,512]{1,0:T(8,128)S(1)} %get-tuple-element.539, ...), kind=kLoop, calls=%fused_computation.12.clone.1 | loop fusion | flops 92258304 | bytes 376832 | tf_op jit(solution)/shard_map/while/body/eval_jaxpr/reduce_sum | solution.py:43
  572.9 14.7 %multiply_reduce_fusion.10 = (f32[8,512]{1,0:T(8,128)S(1)}, f32[8,512]{1,0:T(8,128)S(1)}, f32[8,512]{1,0:T(8,128)S(1)}, f32[8,512]{1,0:T(8,128)S(1)}) fusion(f32[8,512]{1,0:T(8,128)S(1)} %bitcast.380, f32[8,512]{1,0:T(8,128)S(1)} %bitcast.382, f32[8,512]{1,0:T(8,128)S(1)} %bitcast.384, f32[8,512]{1,0:T(8,128)S(1)} %bitcast.385, ...), kind=kLoop, calls=%fused_computation.8.clone.1 | loop fusion | flops 92258304 | bytes 376832 | tf_op jit(solution)/shard_map/while/body/eval_jaxpr/reduce_sum | solution.py:43
  595.2 14.7 %multiply_reduce_fusion.11 = (f32[8,512]{1,0:T(8,128)S(1)}, f32[8,512]{1,0:T(8,128)S(1)}, f32[8,512]{1,0:T(8,128)S(1)}, f32[8,512]{1,0:T(8,128)S(1)}) fusion(f32[8,512]{1,0:T(8,128)S(1)} %bitcast.375, f32[8,512]{1,0:T(8,128)S(1)} %get-tuple-element.538, f32[8,512]{1,0:T(8,128)S(1)} %bitcast.376, f32[8,512]{1,0:T(8,128)S(1)} %get-tuple-element.539, ...), kind=kLoop, calls=%fused_computation.12.clone.1 | loop fusion | flops 92258304 | bytes 376832 | tf_op jit(solution)/shard_map/while/body/eval_jaxpr/reduce_sum | solution.py:43
  610.4 14.7 %multiply_reduce_fusion.10 = (f32[8,512]{1,0:T(8,128)S(1)}, f32[8,512]{1,0:T(8,128)S(1)}, f32[8,512]{1,0:T(8,128)S(1)}, f32[8,512]{1,0:T(8,128)S(1)}) fusion(f32[8,512]{1,0:T(8,128)S(1)} %bitcast.380, f32[8,512]{1,0:T(8,128)S(1)} %bitcast.382, f32[8,512]{1,0:T(8,128)S(1)} %bitcast.384, f32[8,512]{1,0:T(8,128)S(1)} %bitcast.385, ...), kind=kLoop, calls=%fused_computation.8.clone.1 | loop fusion | flops 92258304 | bytes 376832 | tf_op jit(solution)/shard_map/while/body/eval_jaxpr/reduce_sum | solution.py:43
  632.6 14.7 %multiply_reduce_fusion.11 = (f32[8,512]{1,0:T(8,128)S(1)}, f32[8,512]{1,0:T(8,128)S(1)}, f32[8,512]{1,0:T(8,128)S(1)}, f32[8,512]{1,0:T(8,128)S(1)}) fusion(f32[8,512]{1,0:T(8,128)S(1)} %bitcast.375, f32[8,512]{1,0:T(8,128)S(1)} %get-tuple-element.538, f32[8,512]{1,0:T(8,128)S(1)} %bitcast.376, f32[8,512]{1,0:T(8,128)S(1)} %get-tuple-element.539, ...), kind=kLoop, calls=%fused_computation.12.clone.1 | loop fusion | flops 92258304 | bytes 376832 | tf_op jit(solution)/shard_map/while/body/eval_jaxpr/reduce_sum | solution.py:43
  647.8 14.7 %multiply_reduce_fusion.10 = (f32[8,512]{1,0:T(8,128)S(1)}, f32[8,512]{1,0:T(8,128)S(1)}, f32[8,512]{1,0:T(8,128)S(1)}, f32[8,512]{1,0:T(8,128)S(1)}) fusion(f32[8,512]{1,0:T(8,128)S(1)} %bitcast.380, f32[8,512]{1,0:T(8,128)S(1)} %bitcast.382, f32[8,512]{1,0:T(8,128)S(1)} %bitcast.384, f32[8,512]{1,0:T(8,128)S(1)} %bitcast.385, ...), kind=kLoop, calls=%fused_computation.8.clone.1 | loop fusion | flops 92258304 | bytes 376832 | tf_op jit(solution)/shard_map/while/body/eval_jaxpr/reduce_sum | solution.py:43
  670.1 14.7 %multiply_reduce_fusion.11 = (f32[8,512]{1,0:T(8,128)S(1)}, f32[8,512]{1,0:T(8,128)S(1)}, f32[8,512]{1,0:T(8,128)S(1)}, f32[8,512]{1,0:T(8,128)S(1)}) fusion(f32[8,512]{1,0:T(8,128)S(1)} %bitcast.375, f32[8,512]{1,0:T(8,128)S(1)} %get-tuple-element.538, f32[8,512]{1,0:T(8,128)S(1)} %bitcast.376, f32[8,512]{1,0:T(8,128)S(1)} %get-tuple-element.539, ...), kind=kLoop, calls=%fused_computation.12.clone.1 | loop fusion | flops 92258304 | bytes 376832 | tf_op jit(solution)/shard_map/while/body/eval_jaxpr/reduce_sum | solution.py:43
  685.3 14.7 %multiply_reduce_fusion.10 = (f32[8,512]{1,0:T(8,128)S(1)}, f32[8,512]{1,0:T(8,128)S(1)}, f32[8,512]{1,0:T(8,128)S(1)}, f32[8,512]{1,0:T(8,128)S(1)}) fusion(f32[8,512]{1,0:T(8,128)S(1)} %bitcast.380, f32[8,512]{1,0:T(8,128)S(1)} %bitcast.382, f32[8,512]{1,0:T(8,128)S(1)} %bitcast.384, f32[8,512]{1,0:T(8,128)S(1)} %bitcast.385, ...), kind=kLoop, calls=%fused_computation.8.clone.1 | loop fusion | flops 92258304 | bytes 376832 | tf_op jit(solution)/shard_map/while/body/eval_jaxpr/reduce_sum | solution.py:43
  707.5 14.7 %multiply_reduce_fusion.11 = (f32[8,512]{1,0:T(8,128)S(1)}, f32[8,512]{1,0:T(8,128)S(1)}, f32[8,512]{1,0:T(8,128)S(1)}, f32[8,512]{1,0:T(8,128)S(1)}) fusion(f32[8,512]{1,0:T(8,128)S(1)} %bitcast.375, f32[8,512]{1,0:T(8,128)S(1)} %get-tuple-element.538, f32[8,512]{1,0:T(8,128)S(1)} %bitcast.376, f32[8,512]{1,0:T(8,128)S(1)} %get-tuple-element.539, ...), kind=kLoop, calls=%fused_computation.12.clone.1 | loop fusion | flops 92258304 | bytes 376832 | tf_op jit(solution)/shard_map/while/body/eval_jaxpr/reduce_sum | solution.py:43
  722.7 14.7 %multiply_reduce_fusion.10 = (f32[8,512]{1,0:T(8,128)S(1)}, f32[8,512]{1,0:T(8,128)S(1)}, f32[8,512]{1,0:T(8,128)S(1)}, f32[8,512]{1,0:T(8,128)S(1)}) fusion(f32[8,512]{1,0:T(8,128)S(1)} %bitcast.380, f32[8,512]{1,0:T(8,128)S(1)} %bitcast.382, f32[8,512]{1,0:T(8,128)S(1)} %bitcast.384, f32[8,512]{1,0:T(8,128)S(1)} %bitcast.385, ...), kind=kLoop, calls=%fused_computation.8.clone.1 | loop fusion | flops 92258304 | bytes 376832 | tf_op jit(solution)/shard_map/while/body/eval_jaxpr/reduce_sum | solution.py:43
  744.9 14.7 %multiply_reduce_fusion.11 = (f32[8,512]{1,0:T(8,128)S(1)}, f32[8,512]{1,0:T(8,128)S(1)}, f32[8,512]{1,0:T(8,128)S(1)}, f32[8,512]{1,0:T(8,128)S(1)}) fusion(f32[8,512]{1,0:T(8,128)S(1)} %bitcast.375, f32[8,512]{1,0:T(8,128)S(1)} %get-tuple-element.538, f32[8,512]{1,0:T(8,128)S(1)} %bitcast.376, f32[8,512]{1,0:T(8,128)S(1)} %get-tuple-element.539, ...), kind=kLoop, calls=%fused_computation.12.clone.1 | loop fusion | flops 92258304 | bytes 376832 | tf_op jit(solution)/shard_map/while/body/eval_jaxpr/reduce_sum | solution.py:43
  760.2 14.7 %multiply_reduce_fusion.10 = (f32[8,512]{1,0:T(8,128)S(1)}, f32[8,512]{1,0:T(8,128)S(1)}, f32[8,512]{1,0:T(8,128)S(1)}, f32[8,512]{1,0:T(8,128)S(1)}) fusion(f32[8,512]{1,0:T(8,128)S(1)} %bitcast.380, f32[8,512]{1,0:T(8,128)S(1)} %bitcast.382, f32[8,512]{1,0:T(8,128)S(1)} %bitcast.384, f32[8,512]{1,0:T(8,128)S(1)} %bitcast.385, ...), kind=kLoop, calls=%fused_computation.8.clone.1 | loop fusion | flops 92258304 | bytes 376832 | tf_op jit(solution)/shard_map/while/body/eval_jaxpr/reduce_sum | solution.py:43
  782.4 14.7 %multiply_reduce_fusion.11 = (f32[8,512]{1,0:T(8,128)S(1)}, f32[8,512]{1,0:T(8,128)S(1)}, f32[8,512]{1,0:T(8,128)S(1)}, f32[8,512]{1,0:T(8,128)S(1)}) fusion(f32[8,512]{1,0:T(8,128)S(1)} %bitcast.375, f32[8,512]{1,0:T(8,128)S(1)} %get-tuple-element.538, f32[8,512]{1,0:T(8,128)S(1)} %bitcast.376, f32[8,512]{1,0:T(8,128)S(1)} %get-tuple-element.539, ...), kind=kLoop, calls=%fused_computation.12.clone.1 | loop fusion | flops 92258304 | bytes 376832 | tf_op jit(solution)/shard_map/while/body/eval_jaxpr/reduce_sum | solution.py:43
  797.6 14.7 %multiply_reduce_fusion.10 = (f32[8,512]{1,0:T(8,128)S(1)}, f32[8,512]{1,0:T(8,128)S(1)}, f32[8,512]{1,0:T(8,128)S(1)}, f32[8,512]{1,0:T(8,128)S(1)}) fusion(f32[8,512]{1,0:T(8,128)S(1)} %bitcast.380, f32[8,512]{1,0:T(8,128)S(1)} %bitcast.382, f32[8,512]{1,0:T(8,128)S(1)} %bitcast.384, f32[8,512]{1,0:T(8,128)S(1)} %bitcast.385, ...), kind=kLoop, calls=%fused_computation.8.clone.1 | loop fusion | flops 92258304 | bytes 376832 | tf_op jit(solution)/shard_map/while/body/eval_jaxpr/reduce_sum | solution.py:43
  (532 shorter events, 87.3 us)
Async XLA Ops:
  6.5 185.6 %copy-start = (f32[8,121,121]{2,0,1:T(8,128)S(1)}, f32[8,121,121]{2,0,1:T(8,128)}, u32[]{:S(2)}) copy-start(f32[8,121,121]{2,0,1:T(8,128)} %param.21) | copy-start | bytes 1405540
  9.4 60.0 %copy-start.4 = (f32[32768]{0:T(1024)S(1)}, f32[32768]{0:T(1024)}, u32[]{:S(2)}) copy-start(f32[32768]{0:T(1024)} %param.17) | copy-start | bytes 393220
  69.4 23.4 %copy-start.1 = (f32[121,64,512]{2,1,0:T(8,128)}, f32[121,64,512]{2,1,0:T(8,128)S(1)}, u32[]{:S(2)}) copy-start(f32[121,64,512]{2,1,0:T(8,128)S(1)} %add_cosine_fusion) | copy-start | bytes 47579140
  69.4 33.1 %copy-start.2 = (f32[3,32768]{1,0:T(4,128)S(1)}, f32[3,32768]{1,0:T(4,128)}, u32[]{:S(2)}) copy-start(f32[3,32768]{1,0:T(4,128)} %param.16) | copy-start | bytes 1179652
  94.9 16.6 %all-to-all-start.2 = ((f32[32,8,2,121]{3,2,1,0:T(2,128)}), f32[32,8,2,121]{3,2,1,0:T(2,128)S(1)}, u32[]{:S(2)}, u32[]{:S(2)}) async-start(f32[32,8,2,121]{3,2,1,0:T(2,128)} %broadcast_multiply_fusion.1), calls=%async_computation.2 | async-start | bytes 524288 | tf_op jit(solution)/shard_map/all_to_all | solution.py:107
  111.4 56.2 %all-to-all-start = ((f32[32,8,2,4,512]{4,3,2,1,0:T(4,128)}), f32[32,8,2,4,512]{4,3,2,1,0:T(4,128)}, u32[]{:S(2)}, u32[]{:S(2)}) async-start(f32[32,8,2,4,512]{4,3,2,1,0:T(4,128)} %broadcast_multiply_fusion), calls=%async_computation | async-start | bytes 8388608 | tf_op jit(solution)/shard_map/all_to_all | solution.py:114
  167.7 19.8 %all-to-all-start.3 = ((f32[32,8,2,121]{3,2,0,1:T(2,128)}), f32[32,8,2,121]{3,2,0,1:T(2,128)S(1)}, u32[]{:S(2)}, u32[]{:S(2)}) async-start(f32[32,8,2,121]{3,2,0,1:T(2,128)} %copy.74), calls=%async_computation.3 | async-start | bytes 524288 | tf_op jit(solution)/shard_map/all_to_all | solution.py:106
  176.2 17.6 %copy-start.7 = (s32[64,32]{0,1:T(8,128)S(1)}, s32[64,32]{0,1:T(8,128)}, u32[]{:S(2)}) copy-start(s32[64,32]{0,1:T(8,128)} %param.24) | copy-start | bytes 24580
  176.2 17.9 %copy-start.8 = (s32[64,32]{0,1:T(8,128)S(1)}, s32[64,32]{0,1:T(8,128)}, u32[]{:S(2)}) copy-start(s32[64,32]{0,1:T(8,128)} %param.25) | copy-start | bytes 24580
  176.2 18.0 %copy-start.3 = (f32[16,121,121]{2,0,1:T(8,128)S(1)}, f32[16,121,121]{2,0,1:T(8,128)}, u32[]{:S(2)}) copy-start(f32[16,121,121]{2,0,1:T(8,128)} %param.20) | copy-start | bytes 2811076
  176.2 19.4 %copy-start.9 = (s32[64,8]{0,1:T(8,128)S(1)}, s32[64,8]{0,1:T(8,128)}, u32[]{:S(2)}) copy-start(s32[64,8]{0,1:T(8,128)} %param.26) | copy-start | bytes 6148
  187.5 319.3 %all-to-all-start.1 = ((f32[32,8,2,4,512]{4,3,2,0,1:T(4,128)}), f32[32,8,2,4,512]{4,3,2,0,1:T(4,128)}, u32[]{:S(2)}, u32[]{:S(2)}) async-start(f32[32,8,2,4,512]{4,3,2,0,1:T(4,128)} %copy.68), calls=%async_computation.1 | async-start | bytes 8388608 | tf_op jit(solution)/shard_map/all_to_all | solution.py:113
  192.0 281.2 %all-reduce.3.cloned.1.call-start = ((), (), s32[]{:S(2)}) async-start(), calls=%async_computation.4 | async-start | bytes 253952
  193.1 0.7 copy-start.5
  506.8 6.8 copy-start.6
Sparse Core Ops, SparseCore 0:
  198.4 274.8 all-reduce.2
where the time goes:
time: 829 us; the launch traced here: 821 us
  waiting for transfers between devices  329 us (40%)
  other arithmetic  318 us (38%)
  local copies, waits for them, and re-layouts  79.8 us (10%)
  matrix products  50 us (6%)
  starting transfers between devices  28.1 us (3%)
  between operations  14 us (2%)
    unnamed x2, waiting for transfers between devices  275 us
    reduce_sum x16, other arithmetic, near_block(): summed = jnp.sum(source[:, 3, None, :] * lax.rsqrt(radius), axis=2)  235 us
    cos x1, other arithmetic, features(): return jnp.cos(TWO_PI * phase_arg + moment_phase[:, None])  56.1 us
    all_to_all x1, waiting for transfers between devices, local(): lax.all_to_all(out_bodies, 'gx', split_axis=0, concat_axis=0, tiled=True)  48 us
    gather x8, local copies, waits for them, and re-layouts, near_step(): pool_bodies[pointers]  25.7 us
    dot_general x1, matrix products, local(): jnp.einsum('klb,lb->lk', harmonic, charge_rows, precision=EXACT_PRECISION)  23.4 us
    dot_general x1, matrix products, local(): jnp.einsum('klb,lk->lb', harmonic, local_exp, precision=EXACT_PRECISION)  22.5 us
    squeeze x24, local copies, waits for them, and re-layouts, local(): lax.map(near_step, (leaf_bodies[:, :3].reshape(leaves // 8, 8, 3, leaf_wi...  17.4 us
  transfers between devices with their start and end apart: 5, of which 3 were waited for; matrix products, arithmetic and copies ran while one was open for 7% of the time, Pallas kernels for 0%

commit v1 on v0

v1 whole, which is shorter than its diff:
```python
import functools
import math

import jax
import jax.numpy as jnp
from jax import lax
from jax.experimental import pallas as pl
from jax.experimental.pallas import tpu as pltpu
from jax.sharding import PartitionSpec as P

F32 = jnp.float32
BF16 = jnp.bfloat16
SOFTENING = 0.01
LEAVES = 64
WIDTH = 512
KPAD = 128
GROUPS = 48
UNROLL = 8
COS = (1.0, -19.73920440673828, 64.93911743164062, -85.45011138916016, 60.16743087768555, -25.96688461303711, 6.527706146240234)


def split2(a):
    high = a.astype(BF16)
    return high, (a - high.astype(F32)).astype(BF16)


def split3(a):
    high = a.astype(BF16).astype(F32)
    rest = a - high
    middle = rest.astype(BF16).astype(F32)
    return high, middle, rest - middle


def dot_nt(a, b):
    return lax.dot_general(a, b, (((1,), (1,)), ((), ())), preferred_element_type=F32)


def dot_nn(a, b):
    return jnp.dot(a, b, preferred_element_type=F32)


def dot3(dot, a, b):
    a_high, a_low = split2(a)
    b_high, b_low = split2(b)
    return dot(a_high, b_high) + (dot(a_high, b_low) + dot(a_low, b_high))


def pad8(record):
    return jnp.concatenate([record, jnp.zeros((4, record.shape[1]), F32)], axis=0)


def right_side(body, centre):
    row = lax.broadcasted_iota(jnp.int32, body.shape, 0)
    point = jnp.where(row < 3, body - centre, 0.0)
    norm = jnp.sum(point * point, axis=0, keepdims=True) + SOFTENING
    high, middle, low = split3(jnp.where(row == 3, norm, -2.0 * point))
    high_one = jnp.where(row == 3, 1.0, high)
    middle_one = jnp.where(row == 3, 1.0, middle)
    return jnp.concatenate([high, middle, high_one, low, high_one, middle_one], axis=0).astype(BF16)


def left_side(body):
    row = lax.broadcasted_iota(jnp.int32, body.shape, 0)
    point = jnp.where(row < 3, body - 0.5, 0.0)
    norm = jnp.sum(point * point, axis=0, keepdims=True)
    high, middle, low = split3(jnp.where(row == 3, norm, point))
    one = jnp.where(row == 3, 1.0, high)
    return jnp.concatenate(
        [
            one,
            one,
            jnp.where(row == 3, high, middle),
            one,
            jnp.where(row == 3, middle, low),
            jnp.where(row == 3, low, middle),
        ],
        axis=0,
    )


def phase_weights(waves):
    waves = pad8(waves)
    row = lax.broadcasted_iota(jnp.int32, waves.shape, 0)
    freq = jnp.where(row < 3, waves, 0.0)
    turn = jnp.sum(jnp.where(row < 3, 0.5 * waves, waves), axis=0, keepdims=True)
    turn = turn - jnp.round(turn)
    high, middle, low = split3(jnp.where(row == 3, turn, -0.5 * freq))
    plain = jnp.where(row == 3, 0.0, high)
    groups = jnp.concatenate(
        [
            plain,
            plain,
            jnp.where(row == 3, high, middle),
            plain,
            jnp.where(row == 3, middle, low),
            jnp.where(row == 3, low, middle),
        ],
        axis=0,
    )
    return groups.T.astype(BF16)


def cosine_turns(turns):
    rest = turns - jnp.round(turns)
    square = rest * rest
    value = jnp.full_like(square, COS[-1])
    for coefficient in COS[-2::-1]:
        value = value * square + coefficient
    return value


def lane_fold(a):
    return (a[:, :128] + a[:, 128:256]) + (a[:, 256:384] + a[:, 384:])


def basis_leaf(body, weights):
    return cosine_turns(dot_nn(weights, right_side(body, 0.5)))


def upward(moments, shift_ref):
    grouped = moments.reshape(8, 8, KPAD).sum(axis=0)
    row = lax.broadcasted_iota(jnp.int32, grouped.shape, 0)
    total = jnp.zeros((8, KPAD), F32)
    for child in range(8):
        total = total + dot3(dot_nt, jnp.where(row == child, grouped, 0.0), shift_ref[child])
    return jnp.sum(total, axis=0, keepdims=True)


def feature_kernel(bodies, waves, shift, harmonic, left, moments, top, transposed):
    weights = phase_weights(waves[...])
    lane = lax.broadcasted_iota(jnp.int32, (KPAD, KPAD), 1)
    transposed[...] = jnp.zeros_like(transposed)

    def step(pair, carry):
        for half in range(2):
            leaf = pair * 2 + half
            body = pad8(bodies[leaf])
            basis = basis_leaf(body, weights)
            harmonic[leaf] = basis
            column = jnp.sum(lane_fold(basis * body[3:4]), axis=1, keepdims=True)
            transposed[...] = jnp.where(lane == leaf, column, transposed[...])
            left[leaf, :, :GROUPS] = left_side(body).T.astype(BF16)
        return carry

    lax.fori_loop(0, LEAVES // 2, step, 0)
    own = transposed[...].T[:LEAVES]
    moments[...] = own
    top[...] = jnp.broadcast_to(upward(own, shift), (8, KPAD))


def offset_vector(code):
    return (
        (code % 3 - 1).astype(F32),
        (code // 3 % 3 - 1).astype(F32),
        (code // 9 - 1).astype(F32),
    )


def source_right(body, shift):
    row = lax.broadcasted_iota(jnp.int32, body.shape, 0)
    shift_x, shift_y, shift_z = offset_vector(shift)
    centre = 0.5 - jnp.where(row == 0, shift_x, jnp.where(row == 1, shift_y, shift_z))
    return right_side(body, centre)


def pair_rows(left, right, charge, start, size):
    value = charge * lax.rsqrt(dot_nn(left[start : start + size], right))
    return lane_fold(value)


def local_expansions(pool_moments, m2l, shift, table, far_index, top_class, expansions):
    rows = pool_moments.shape[0]
    pool_high, pool_low = split2(pool_moments[...])
    for pair in range(8):
        op_high, op_low = split2(m2l[2 * pair : 2 * pair + 2].reshape(256, KPAD))
        moved = dot_nt(pool_high, op_high) + (dot_nt(pool_high, op_low) + dot_nt(pool_low, op_high))
        table[2 * pair * rows : (2 * pair + 1) * rows] = moved[:, :KPAD]
        table[(2 * pair + 1) * rows : (2 * pair + 2) * rows] = moved[:, KPAD:]
    table[16 * rows : 16 * rows + 8] = jnp.zeros((8, KPAD), F32)

    def tree(parts):
        while len(parts) > 1:
            parts = [a + b for a, b in zip(parts[::2], parts[1::2])]
        return parts[0]

    top_local = tree(
        [table[pl.ds(top_class[e] * rows + (rows - 32 + e), 1), :] for e in range(32)]
    )
    top_rows = jnp.broadcast_to(top_local, (8, KPAD))
    row = lax.broadcasted_iota(jnp.int32, (8, KPAD), 0)
    down = jnp.zeros((8, KPAD), F32)
    for child in range(8):
        down = jnp.where(row == child, dot3(dot_nn, top_rows, shift[child]), down)

    def gather(leaf, carry):
        base = leaf * 32
        expansions[pl.ds(leaf, 1), :] = tree(
            [table[pl.ds(far_index[base + e], 1), :] for e in range(32)]
        )
        return carry

    lax.fori_loop(0, LEAVES, gather, 0)
    return (expansions[...].reshape(8, 8, KPAD) + down[None]).reshape(LEAVES, KPAD)


def finish_kernel(
    count, codes, far_index, top_list, top_class,
    left, m2l, shift, own_moments, in_moments, tops,
    harmonic_hbm, bodies_hbm, in_bodies_hbm,
    out,
    pool, harmonic, near, pool_moments, table, expansions, sems,
):
    slots = in_bodies_hbm.shape[0]
    copy_own = pltpu.make_async_copy(bodies_hbm, pool.at[pl.ds(0, LEAVES)], sems.at[0])
    copy_in = pltpu.make_async_copy(in_bodies_hbm, pool.at[pl.ds(LEAVES, slots)], sems.at[1])
    copy_harmonic = pltpu.make_async_copy(harmonic_hbm, harmonic, sems.at[2])
    copy_own.start()
    copy_in.start()
    copy_harmonic.start()
    near[...] = jnp.zeros_like(near)
    rows = LEAVES + slots
    pool_moments[:LEAVES] = own_moments[...]
    pool_moments[LEAVES:rows] = in_moments[...]
    for e in range(32):
        pool_moments[rows + e : rows + e + 1, :] = tops[pl.ds(top_list[e], 1), :]
    local = local_expansions(pool_moments, m2l, shift, table, far_index, top_class, expansions)
    local_columns = jnp.concatenate([local, jnp.zeros((KPAD - LEAVES, KPAD), F32)], axis=0).T

    copy_own.wait()
    copy_in.wait()

    def near_step(group, carry):
        for member in range(UNROLL):
            code = codes[group * UNROLL + member]
            target = code & 63
            source = (code >> 6) & 1023
            live = (code >> 21).astype(F32)
            body = pad8(pool[source])
            right = source_right(body, (code >> 16) & 31)
            charge = body[3:4] * live
            for start in range(0, WIDTH, 128):
                near[target, start : start + 128] += pair_rows(
                    left.at[target][:, :GROUPS], right, charge, start, 128
                )
        return carry

    lax.fori_loop(0, (count[0] + UNROLL - 1) // UNROLL, near_step, 0)
    copy_harmonic.wait()
    ones = jnp.ones((8, 128), BF16)

    def far_step(group, columns):
        for member in range(8):
            leaf = group * 8 + member
            product = harmonic[leaf] * columns[:, member : member + 1]
            far = jnp.sum(product, axis=0, keepdims=True)
            near_high, near_low = split2(near[leaf])
            total = dot_nt(ones, near_high) + dot_nt(ones, near_low)
            out[pl.ds(leaf, 1), :] = total[:1] + far
        return pltpu.roll(columns, KPAD - 8, 1)

    lax.fori_loop(0, LEAVES // 8, far_step, local_columns)


def near_codes(near_src, near_shift, wanted):
    number = near_src.size
    flat = near_src.reshape(number)
    entry = jnp.arange(number, dtype=jnp.int32)
    code = (entry // near_src.shape[1]) + flat * 64 + near_shift.reshape(number) * 65536 + (1 << 21)
    wanted = wanted.reshape(number)
    place = jnp.sum(wanted[None, :] & (entry[None, :] < entry[:, None]), axis=1, dtype=jnp.int32)
    place = jnp.where(wanted, place, -1)
    codes = jnp.sum(jnp.where(place[None, :] == entry[:, None], code[None, :], 0), axis=1)
    return codes, jnp.sum(wanted, dtype=jnp.int32)[None]


SMEM = pl.BlockSpec(memory_space=pltpu.SMEM)
VMEM = pl.BlockSpec(memory_space=pltpu.VMEM)
ANY = pl.BlockSpec(memory_space=pl.ANY)


def pad_ops(ops):
    return jnp.pad(ops, ((0, 0), (0, KPAD - ops.shape[1]), (0, KPAD - ops.shape[2])))


def wave_rows(moment_freq, moment_phase):
    rows = jnp.concatenate([moment_freq, moment_phase[None] * (0.5 / math.pi)], axis=0)
    return jnp.pad(rows, ((0, 0), (0, KPAD - rows.shape[1])))


def run_features(bodies, waves, shift):
    return pl.pallas_call(
        feature_kernel,
        out_shape=[
            jax.ShapeDtypeStruct((LEAVES, KPAD, WIDTH), F32),
            jax.ShapeDtypeStruct((LEAVES, WIDTH, 128), BF16),
            jax.ShapeDtypeStruct((LEAVES, KPAD), F32),
            jax.ShapeDtypeStruct((8, KPAD), F32),
        ],
        in_specs=[VMEM] * 3,
        out_specs=[VMEM] * 4,
        scratch_shapes=[pltpu.VMEM((KPAD, KPAD), F32)],
        compiler_params=pltpu.CompilerParams(vmem_limit_bytes=60 << 20),
        cost_estimate=pl.CostEstimate(flops=20_000_000_000, bytes_accessed=30_000_000, transcendentals=0),
    )(bodies, waves, shift)


def run_finish(count, codes, far_index, top_list, top_class, left, m2l, shift, moments, in_moments, tops, harmonic, bodies, in_bodies):
    slots = in_bodies.shape[0]
    rows = LEAVES + slots + 32
    return pl.pallas_call(
        finish_kernel,
        out_shape=jax.ShapeDtypeStruct((LEAVES, WIDTH), F32),
        in_specs=[SMEM] * 5 + [VMEM] * 6 + [ANY] * 3,
        out_specs=VMEM,
        scratch_shapes=[
            pltpu.VMEM((LEAVES + slots, 4, WIDTH), F32),
            pltpu.VMEM((LEAVES, KPAD, WIDTH), F32),
            pltpu.VMEM((LEAVES, WIDTH, 128), F32),
            pltpu.VMEM((rows, KPAD), F32),
            pltpu.VMEM((16 * rows + 8, KPAD), F32),
            pltpu.VMEM((LEAVES, KPAD), F32),
            pltpu.SemaphoreType.DMA((3,)),
        ],
        compiler_params=pltpu.CompilerParams(vmem_limit_bytes=62 << 20),
        cost_estimate=pl.CostEstimate(flops=60_000_000_000, bytes_accessed=40_000_000, transcendentals=0),
    )(count, codes, far_index, top_list, top_class, left, m2l, shift, moments, in_moments, tops, harmonic, bodies, in_bodies)


def exchange(values):
    values = lax.all_to_all(values, "gx", split_axis=0, concat_axis=0, tiled=True)
    return lax.all_to_all(values, "gy", split_axis=1, concat_axis=1, tiled=True)


def local(
    positions,
    charges,
    moment_freq,
    moment_phase,
    m2l_ops,
    child_parent_shift_matrix,
    send_leaf,
    send_count,
    far_src,
    far_class,
    near_src,
    near_shift,
    top_list,
    top_class,
):
    leaves = far_src.shape[0]
    peers, slot_count = send_leaf.shape[1:]
    coarse_size = lax.axis_size("gx")
    fine_size = lax.axis_size("gy")
    bodies = (
        jnp.concatenate([positions, charges[None, :]], axis=0)
        .reshape(4, leaves, WIDTH)
        .transpose(1, 0, 2)
    )
    chosen = send_leaf[0]
    in_bodies = exchange(
        bodies[chosen].reshape(coarse_size, fine_size, slot_count, 4, WIDTH)
    ).reshape(peers * slot_count, 4, WIDTH)
    waves = wave_rows(moment_freq, moment_phase)
    shift = pad_ops(child_parent_shift_matrix)
    m2l = pad_ops(m2l_ops)
    harmonic, left, moments, top = run_features(bodies, waves, shift)
    sent = jnp.concatenate(
        [moments[chosen], jnp.broadcast_to(top[:1][None], (peers, 1, KPAD))], axis=1
    )
    came = exchange(sent.reshape(coarse_size, fine_size, slot_count + 1, KPAD)).reshape(
        peers, slot_count + 1, KPAD
    )
    in_moments = came[:, :slot_count].reshape(peers * slot_count, KPAD)
    tops = came[:, slot_count]
    codes, count = near_codes(near_src, near_shift, near_src >= 0)
    rows = leaves + peers * slot_count + 32
    far_index = jnp.where(far_src >= 0, far_class * rows + far_src, 16 * rows).reshape(-1)
    result = run_finish(
        count, codes, far_index, top_list[0], top_class[0], left, m2l, shift,
        moments, in_moments, tops, harmonic, bodies, in_bodies,
    )
    return result.reshape(leaves * WIDTH)


def solution(mesh):
    placed = (
        P(None, ("gx", "gy")),
        P(("gx", "gy")),
        P(),
        P(),
        P(),
        P(),
        P(("gx", "gy"), None, None),
        P(("gx", "gy"), None),
        P(("gx", "gy"), None),
        P(("gx", "gy"), None),
        P(("gx", "gy"), None),
        P(("gx", "gy"), None),
        P(("gx", "gy"), None),
        P(("gx", "gy"), None),
    )
    return jax.shard_map(
        local, mesh=mesh, in_specs=placed, out_specs=P(("gx", "gy")), check_vma=False
    )
```

time: 829 us -> 320 us (0.39)
  other arithmetic: 318 us -> 6.48 us
  waiting for transfers between devices: 329 us -> 151 us
  Pallas kernels: 0 us -> 103 us
  local copies, waits for them, and re-layouts: 79.8 us -> 28.3 us
  matrix products: 50 us -> 0 us
  between operations: 14 us -> 0.19 us
    unnamed x2 -> x0, waiting for transfers between devices: 275 us -> none
    reduce_sum x17 -> x3, other arithmetic: 235 us -> 1.64 us  [the longest x1 0.78 us: near_codes(): jnp.sum(jnp.where(place[None, :] == entry[:, None], code[None, :], 0), ax...]
    pallas_call x0 -> x2, Pallas kernels: none -> 103 us  [the longest x1 73.9 us: run_finish(): pl.pallas_call(finish_kernel, out_shape=jax.ShapeDtypeStruct((LEAVES, WID...]
    all_to_all x4, waiting for transfers between devices: 53.7 us -> 151 us  [the longest x2 100 us: exchange(): return lax.all_to_all(values, 'gy', split_axis=1, concat_axis=1, tiled=True)]
    cos x1 -> x0, other arithmetic: 56.1 us -> none  [features(): return jnp.cos(TWO_PI * phase_arg + moment_phase[:, None])]
    dot_general x8 -> x0, matrix products: 50 us -> none  [the longest x1 23.4 us: local(): jnp.einsum('klb,lb->lk', harmonic, charge_rows, precision=EXACT_PRECISION)]
    gather x12 -> x3, local copies, waits for them, and re-layouts: 37.5 us -> 6.45 us  [the longest x1 4.65 us: local(): bodies[chosen].reshape(coarse_size, fine_size, slot_count, 4, WIDTH)]
    squeeze x32 -> x1, local copies, waits for them, and re-layouts: 17.7 us -> 0.66 us  [local(): tops = came[:, slot_count]]
  transfers between devices with their start and end apart: 5 -> 4, of which waited for: 3 -> 4; matrix products, arithmetic and copies ran while one was open for 7% -> 5% of each run, Pallas kernels for 0% -> 0%
where the time goes in v1:
time: 320 us; the launch traced here: 317 us
  waiting for transfers between devices  151 us (47%)
  Pallas kernels  103 us (32%)
  local copies, waits for them, and re-layouts  28.3 us (9%)
  starting transfers between devices  27.6 us (9%)
  other arithmetic  6.48 us (2%)
    all_to_all x2, waiting for transfers between devices, exchange(): return lax.all_to_all(values, 'gy', split_axis=1, concat_axis=1, tiled=True)  100 us
    pallas_call x1, Pallas kernels, run_finish(): pl.pallas_call(finish_kernel, out_shape=jax.ShapeDtypeStruct((LEAVES, WID...  73.9 us
    all_to_all x2, waiting for transfers between devices, exchange(): lax.all_to_all(values, 'gx', split_axis=0, concat_axis=0, tiled=True)  51.3 us
    pallas_call x1, Pallas kernels, run_features(): pl.pallas_call(feature_kernel, out_shape=[jax.ShapeDtypeStruct((LEAVES, K...  28.8 us
    all_to_all x2, starting transfers between devices, exchange(): lax.all_to_all(values, 'gx', split_axis=0, concat_axis=0, tiled=True)  14.5 us
    all_to_all x2, starting transfers between devices, exchange(): return lax.all_to_all(values, 'gy', split_axis=1, concat_axis=1, tiled=True)  13 us
  transfers between devices with their start and end apart: 4, of which 4 were waited for; matrix products, arithmetic and copies ran while one was open for 5% of the time, Pallas kernels for 0%

profile of v1, /device:TPU:6, one launch (start us, length us, event | category | flops | bytes accessed | tf_op | source)
XLA Modules:
  0.0 316.6 jit_solution(4669083825555123102)
XLA Ops:
  0.0 0.7 multiply_bitcast_fusion
  0.7 0.7 compare_select_fusion
  1.6 1.1 copy.70
  2.8 1.3 select_maximum_fusion.waves
  4.1 2.2 maximum_bitcast_fusion.bodies.bodies_hbm
  6.2 0.8 pad.13.shift
  7.1 28.8 %shard_map.127 = (f32[64,128,512]{2,1,0:T(8,128)}, bf16[64,512,128]{2,1,0:T(8,128)(2,1)}, f32[64,128]{1,0:T(8,128)}, f32[8,128]{1,0:T(8,128)}) custom-call(f32[64,4,512]{2,1,0:T(4,128)} %maximum_bitcast_fusion.bodies.bodies_hbm, f32[4,128]{1,0:T(4,128)} %select_maximum_fusion.waves, f32[8,128,128]{2,1,0:T(8,128)} %pad.13.shift), custom_call_target="tpu_custom_call" | custom-call | flops 20000000000 | bytes 30000000 | tf_op jit(solution)/shard_map/pallas_call | solution.py:291
  35.9 0.7 slice_bitcast_fusion.1
  36.7 1.8 gather_fusion
  38.5 0.8 copy.74
  39.3 7.6 %all-to-all-start = ((f32[32,8,3,128]{3,1,2,0:T(8,128)}), f32[32,8,3,128]{3,1,2,0:T(8,128)S(1)}, u32[]{:S(2)}, u32[]{:S(2)}) async-start(f32[32,8,3,128]{3,1,2,0:T(8,128)} %copy.74), calls=%async_computation | async-start | bytes 786432 | tf_op jit(solution)/shard_map/all_to_all | solution.py:330
  46.9 4.6 %gather_fusion.1 = f32[512,4,512]{2,1,0:T(4,128)} fusion(f32[64,4,512]{2,1,0:T(4,128)S(1)} %copy-done, s32[1024]{0:T(1024)S(1)} %pad_clamp_fusion), kind=kCustom, calls=%fused_computation.1 | custom fusion | bytes 8390656 | tf_op jit(solution)/shard_map/gather | solution.py:361
  51.6 3.4 %all-to-all-done = f32[32,8,3,128]{3,1,2,0:T(8,128)S(1)} async-done(((f32[32,8,3,128]{3,1,2,0:T(8,128)}), f32[32,8,3,128]{3,1,2,0:T(8,128)S(1)}, u32[]{:S(2)}, u32[]{:S(2)}) %all-to-all-start) | async-done | bytes 393248 | tf_op jit(solution)/shard_map/all_to_all | solution.py:330
  55.0 7.0 %all-to-all-start.2 = ((f32[32,8,2,4,512]{4,3,2,1,0:T(4,128)}), f32[32,8,2,4,512]{4,3,2,1,0:T(4,128)}, u32[]{:S(2)}, u32[]{:S(2)}) async-start(f32[32,8,2,4,512]{4,3,2,1,0:T(4,128)} %bitcast.28), calls=%async_computation.2 | async-start | bytes 8388608 | tf_op jit(solution)/shard_map/all_to_all | solution.py:330
  61.9 0.8 copy.75
  62.8 47.9 %all-to-all-done.2 = f32[32,8,2,4,512]{4,3,2,1,0:T(4,128)} async-done(((f32[32,8,2,4,512]{4,3,2,1,0:T(4,128)}), f32[32,8,2,4,512]{4,3,2,1,0:T(4,128)}, u32[]{:S(2)}, u32[]{:S(2)}) %all-to-all-start.2) | async-done | bytes 4194336 | tf_op jit(solution)/shard_map/all_to_all | solution.py:330
  110.7 8.5 %all-to-all-start.1 = ((f32[32,8,3,128]{3,0,2,1:T(8,128)}), f32[32,8,3,128]{3,0,2,1:T(8,128)S(1)}, u32[]{:S(2)}, u32[]{:S(2)}) async-start(f32[32,8,3,128]{3,0,2,1:T(8,128)} %copy.75), calls=%async_computation.1 | async-start | bytes 786432 | tf_op jit(solution)/shard_map/all_to_all | solution.py:331
  119.2 5.5 %copy.78 = f32[32,8,2,4,512]{4,3,2,0,1:T(4,128)} copy(f32[32,8,2,4,512]{4,3,2,1,0:T(4,128)} %all-to-all-done.2) | data formatting | bytes 8388608 | tf_op jit(solution)/shard_map/all_to_all | solution.py:330
  124.7 8.7 %all-to-all-done.1 = f32[32,8,3,128]{3,0,2,1:T(8,128)S(1)} async-done(((f32[32,8,3,128]{3,0,2,1:T(8,128)}), f32[32,8,3,128]{3,0,2,1:T(8,128)S(1)}, u32[]{:S(2)}, u32[]{:S(2)}) %all-to-all-start.1) | async-done | bytes 393248 | tf_op jit(solution)/shard_map/all_to_all | solution.py:331
  133.4 4.6 %all-to-all-start.3 = ((f32[32,8,2,4,512]{4,3,2,0,1:T(4,128)}), f32[32,8,2,4,512]{4,3,2,0,1:T(4,128)}, u32[]{:S(2)}, u32[]{:S(2)}) async-start(f32[32,8,2,4,512]{4,3,2,0,1:T(4,128)} %copy.78), calls=%async_computation.3 | async-start | bytes 8388608 | tf_op jit(solution)/shard_map/all_to_all | solution.py:331
  138.0 0.7 convert_reduce_fusion.1
  139.1 0.7 reshape.101.far_index
  140.1 0.3 copy.71
  140.4 1.1 pad.14.m2l
  141.7 0.8 select_reduce_fusion.codes
  142.5 0.2 copy.82
  142.8 0.9 copy.77
  143.7 0.7 slice_bitcast_fusion.tops
  144.3 91.3 %all-to-all-done.3 = f32[32,8,2,4,512]{4,3,2,0,1:T(4,128)} async-done(((f32[32,8,2,4,512]{4,3,2,0,1:T(4,128)}), f32[32,8,2,4,512]{4,3,2,0,1:T(4,128)}, u32[]{:S(2)}, u32[]{:S(2)}) %all-to-all-start.3) | async-done | bytes 4194336 | tf_op jit(solution)/shard_map/all_to_all | solution.py:331
  235.6 5.5 %copy.79 = f32[32,8,2,4,512]{4,3,2,1,0:T(4,128)} copy(f32[32,8,2,4,512]{4,3,2,0,1:T(4,128)} %all-to-all-done.3) | data formatting | bytes 8388608 | tf_op jit(solution)/shard_map/all_to_all | solution.py:331
  241.2 73.9 %shard_map.128 = f32[64,512]{1,0:T(8,128)} custom-call(s32[1]{0:T(128)} %bitcast.count, s32[512]{0:T(512)} %select_reduce_fusion.codes, s32[2048]{0:T(1024)} %reshape.101.far_index, s32[32]{0:T(128)} %bitcast.37, s32[32]{0:T(128)} %bitcast.38, bf16[64,512,128]{2,1,0:T(8,128)(2,1)} %get-tuple-element.9.left, f32[16,128,128]{2,1,0:T(8,128)} %pad.14.m2l, ...), custom_call_target="tpu_custom_call" | custom-call | flops 60000002048 | bytes 40000000 | tf_op jit(solution)/shard_map/pallas_call | solution.py:310
  315.0 1.6 copy.80
  (30 shorter events, 1.2 us)
Async XLA Ops:
  35.9 11.0 %copy-start = (f32[64,4,512]{2,1,0:T(4,128)S(1)}, f32[64,4,512]{2,1,0:T(4,128)}, u32[]{:S(2)}) copy-start(f32[64,4,512]{2,1,0:T(4,128)} %maximum_bitcast_fusion.bodies.bodies_hbm) | copy-start | bytes 1572868
  39.3 15.6 %all-to-all-start = ((f32[32,8,3,128]{3,1,2,0:T(8,128)}), f32[32,8,3,128]{3,1,2,0:T(8,128)S(1)}, u32[]{:S(2)}, u32[]{:S(2)}) async-start(f32[32,8,3,128]{3,1,2,0:T(8,128)} %copy.74), calls=%async_computation | async-start | bytes 786432 | tf_op jit(solution)/shard_map/all_to_all | solution.py:330
  55.0 55.7 %all-to-all-start.2 = ((f32[32,8,2,4,512]{4,3,2,1,0:T(4,128)}), f32[32,8,2,4,512]{4,3,2,1,0:T(4,128)}, u32[]{:S(2)}, u32[]{:S(2)}) async-start(f32[32,8,2,4,512]{4,3,2,1,0:T(4,128)} %bitcast.28), calls=%async_computation.2 | async-start | bytes 8388608 | tf_op jit(solution)/shard_map/all_to_all | solution.py:330
  110.7 22.7 %all-to-all-start.1 = ((f32[32,8,3,128]{3,0,2,1:T(8,128)}), f32[32,8,3,128]{3,0,2,1:T(8,128)S(1)}, u32[]{:S(2)}, u32[]{:S(2)}) async-start(f32[32,8,3,128]{3,0,2,1:T(8,128)} %copy.75), calls=%async_computation.1 | async-start | bytes 786432 | tf_op jit(solution)/shard_map/all_to_all | solution.py:331
  124.7 13.4 %copy-start.4 = (s32[64,8]{0,1:T(8,128)S(1)}, s32[64,8]{0,1:T(8,128)}, u32[]{:S(2)}) copy-start(s32[64,8]{0,1:T(8,128)} %param.23) | copy-start | bytes 6148
  124.7 14.3 %copy-start.2 = (s32[64,32]{0,1:T(8,128)S(1)}, s32[64,32]{0,1:T(8,128)}, u32[]{:S(2)}) copy-start(s32[64,32]{0,1:T(8,128)} %param.21) | copy-start | bytes 24580
  124.7 14.3 %copy-start.3 = (s32[64,32]{0,1:T(8,128)S(1)}, s32[64,32]{0,1:T(8,128)}, u32[]{:S(2)}) copy-start(s32[64,32]{0,1:T(8,128)} %param.22) | copy-start | bytes 24580
  124.7 15.1 %copy-start.5 = (s32[64,8]{0,1:T(8,128)S(1)}, s32[64,8]{0,1:T(8,128)}, u32[]{:S(2)}) copy-start(s32[64,8]{0,1:T(8,128)} %param.24) | copy-start | bytes 6148
  124.7 15.4 %copy-start.1 = (f32[16,121,121]{2,0,1:T(8,128)S(1)}, f32[16,121,121]{2,0,1:T(8,128)}, u32[]{:S(2)}) copy-start(f32[16,121,121]{2,0,1:T(8,128)} %param.18) | copy-start | bytes 2811076
  133.4 102.2 %all-to-all-start.3 = ((f32[32,8,2,4,512]{4,3,2,0,1:T(4,128)}), f32[32,8,2,4,512]{4,3,2,0,1:T(4,128)}, u32[]{:S(2)}, u32[]{:S(2)}) async-start(f32[32,8,2,4,512]{4,3,2,0,1:T(4,128)} %copy.78), calls=%async_computation.3 | async-start | bytes 8388608 | tf_op jit(solution)/shard_map/all_to_all | solution.py:331

commit v2 on v1

--- a/solution.py
+++ b/solution.py
@@ -126,28 +126,6 @@
     return jnp.sum(total, axis=0, keepdims=True)
 
 
-def feature_kernel(bodies, waves, shift, harmonic, left, moments, top, transposed):
-    weights = phase_weights(waves[...])
-    lane = lax.broadcasted_iota(jnp.int32, (KPAD, KPAD), 1)
-    transposed[...] = jnp.zeros_like(transposed)
-
-    def step(pair, carry):
-        for half in range(2):
-            leaf = pair * 2 + half
-            body = pad8(bodies[leaf])
-            basis = basis_leaf(body, weights)
-            harmonic[leaf] = basis
-            column = jnp.sum(lane_fold(basis * body[3:4]), axis=1, keepdims=True)
-            transposed[...] = jnp.where(lane == leaf, column, transposed[...])
-            left[leaf, :, :GROUPS] = left_side(body).T.astype(BF16)
-        return carry
-
-    lax.fori_loop(0, LEAVES // 2, step, 0)
-    own = transposed[...].T[:LEAVES]
-    moments[...] = own
-    top[...] = jnp.broadcast_to(upward(own, shift), (8, KPAD))
-
-
 def offset_vector(code):
     return (
         (code % 3 - 1).astype(F32),
@@ -205,7 +183,7 @@
 
 def finish_kernel(
     count, codes, far_index, top_list, top_class,
-    left, m2l, shift, own_moments, in_moments, tops,
+    left, m2l, shift, own_moments, in_rows, near_own,
     harmonic_hbm, bodies_hbm, in_bodies_hbm,
     out,
     pool, harmonic, near, pool_moments, table, expansions, sems,
@@ -220,9 +198,15 @@
     near[...] = jnp.zeros_like(near)
     rows = LEAVES + slots
     pool_moments[:LEAVES] = own_moments[...]
-    pool_moments[LEAVES:rows] = in_moments[...]
+    fine = in_rows.shape[1] // 3
+    for peer in range(in_rows.shape[0]):
+        start = LEAVES + 2 * fine * peer
+        pool_moments[start : start + 2 * fine] = in_rows[peer, : 2 * fine]
     for e in range(32):
-        pool_moments[rows + e : rows + e + 1, :] = tops[pl.ds(top_list[e], 1), :]
+        owner = top_list[e]
+        pool_moments[rows + e : rows + e + 1, :] = in_rows[
+            owner // fine, pl.ds(2 * fine + lax.rem(owner, fine), 1), :
+        ]
     local = local_expansions(pool_moments, m2l, shift, table, far_index, top_class, expansions)
     local_columns = jnp.concatenate([local, jnp.zeros((KPAD - LEAVES, KPAD), F32)], axis=0).T
 
@@ -255,7 +239,7 @@
             far = jnp.sum(product, axis=0, keepdims=True)
             near_high, near_low = split2(near[leaf])
             total = dot_nt(ones, near_high) + dot_nt(ones, near_low)
-            out[pl.ds(leaf, 1), :] = total[:1] + far
+            out[pl.ds(leaf, 1), :] = total[:1] + far + near_own[pl.ds(leaf, 1), :]
         return pltpu.roll(columns, KPAD - 8, 1)
 
     lax.fori_loop(0, LEAVES // 8, far_step, local_columns)
@@ -287,24 +271,7 @@
     return jnp.pad(rows, ((0, 0), (0, KPAD - rows.shape[1])))
 
 
-def run_features(bodies, waves, shift):
-    return pl.pallas_call(
-        feature_kernel,
-        out_shape=[
-            jax.ShapeDtypeStruct((LEAVES, KPAD, WIDTH), F32),
-            jax.ShapeDtypeStruct((LEAVES, WIDTH, 128), BF16),
-            jax.ShapeDtypeStruct((LEAVES, KPAD), F32),
-            jax.ShapeDtypeStruct((8, KPAD), F32),
-        ],
-        in_specs=[VMEM] * 3,
-        out_specs=[VMEM] * 4,
-        scratch_shapes=[pltpu.VMEM((KPAD, KPAD), F32)],
-        compiler_params=pltpu.CompilerParams(vmem_limit_bytes=60 << 20),
-        cost_estimate=pl.CostEstimate(flops=20_000_000_000, bytes_accessed=30_000_000, transcendentals=0),
-    )(bodies, waves, shift)
-
-
-def run_finish(count, codes, far_index, top_list, top_class, left, m2l, shift, moments, in_moments, tops, harmonic, bodies, in_bodies):
+def run_finish(count, codes, far_index, top_list, top_class, left, m2l, shift, moments, in_rows, near_own, harmonic, bodies, in_bodies):
     slots = in_bodies.shape[0]
     rows = LEAVES + slots + 32
     return pl.pallas_call(
@@ -323,12 +290,249 @@
         ],
         compiler_params=pltpu.CompilerParams(vmem_limit_bytes=62 << 20),
         cost_estimate=pl.CostEstimate(flops=60_000_000_000, bytes_accessed=40_000_000, transcendentals=0),
-    )(count, codes, far_index, top_list, top_class, left, m2l, shift, moments, in_moments, tops, harmonic, bodies, in_bodies)
-
-
-def exchange(values):
-    values = lax.all_to_all(values, "gx", split_axis=0, concat_axis=0, tiled=True)
-    return lax.all_to_all(values, "gy", split_axis=1, concat_axis=1, tiled=True)
+    )(count, codes, far_index, top_list, top_class, left, m2l, shift, moments, in_rows, near_own, harmonic, bodies, in_bodies)
+
+
+def exchange_kernel(
+    pairs, bodies, table, waves, shift,
+    in_bodies, in_rows, harmonic_out, left_out, moments, near_own,
+    r1, r2, r3, l1, l2, l3, opposite,
+    packs, harmonic, left, transposed, column_rows, row_pack, tables, table_words,
+    ring_send, ring_recv, small_send, small_recv, plane_send, plane_recv, local_sems, out_sems,
+):
+    gx, gy = lax.axis_index("gx"), lax.axis_index("gy")
+    coarse, fine = row_pack.shape[0], column_rows.shape[0]
+    right = {"gy": lax.rem(gy + 1, fine)}
+    back = {"gy": lax.rem(gy + fine - 1, fine)}
+    half = LEAVES // 2
+
+    barrier = pltpu.get_barrier_semaphore()
+
+    def greet_plane(j, carry):
+        pl.semaphore_signal(barrier, inc=1, device_id={"gx": lax.rem(gx + j, coarse)})
+        return carry
+
+    lax.fori_loop(1, coarse, greet_plane, 0)
+    for k in range(1, fine):
+        pl.semaphore_signal(barrier, inc=1, device_id={"gy": lax.rem(gy + k, fine)})
+    pl.semaphore_wait(barrier, coarse + fine - 2)
+
+    def remote(source, target, send, recv, device):
+        copy = pltpu.make_async_remote_copy(
+            src_ref=source, dst_ref=target, send_sem=send, recv_sem=recv, device_id=device
+        )
+        copy.start()
+        return copy
+
+    def ring(step):
+        if step == 4:
+            return (
+                remote(r3.at[pl.ds(0, half)], opposite.at[pl.ds(0, half)],
+                       ring_send.at[6], ring_recv.at[6], right),
+                remote(l3.at[pl.ds(half, half)], opposite.at[pl.ds(half, half)],
+                       ring_send.at[7], ring_recv.at[7], back),
+            )
+        sources = ((bodies, bodies), (r1, l1), (r2, l2))[step - 1]
+        targets = ((r1, l1), (r2, l2), (r3, l3))[step - 1]
+        slot = 2 * (step - 1)
+        return (
+            remote(sources[0], targets[0], ring_send.at[slot], ring_recv.at[slot], right),
+            remote(sources[1], targets[1], ring_send.at[slot + 1], ring_recv.at[slot + 1], back),
+        )
+
+    first = ring(1)
+    for k in range(1, fine):
+        there = lax.rem(gy + k, fine)
+        remote(table.at[there], tables.at[k], small_send.at[0], small_recv.at[0], {"gy": there})
+    own_table = pltpu.make_async_copy(table.at[gy], tables.at[0], local_sems.at[0])
+    own_table.start()
+    own_table.wait()
+    others = tables.at[pl.ds(1, fine - 1)]
+    pltpu.make_async_copy(others, others, small_recv.at[0]).wait()
+    words = pltpu.make_async_copy(tables, table_words, local_sems.at[0])
+    words.start()
+    words.wait()
+
+    def pack(block, offset):
+        there = lax.rem(gy + fine - offset, fine)
+        buffer = packs.at[offset]
+        place = pl.ds((gx * fine + there) * 2, 2)
+
+        def one(quad, carry):
+            for part in range(4):
+                peer = quad * 4 + part
+                for slot in range(2):
+                    buffer[peer, slot] = block[table_words[offset, 0, peer * 2 + slot]]
+            return carry
+
+        lax.fori_loop(0, coarse // 4, one, 0)
+
+        def push(j, carry):
+            peer = lax.rem(gx + j, coarse)
+            remote(buffer.at[peer], in_bodies.at[place], plane_send.at[0], plane_recv.at[0],
+                   {"gx": peer})
+            return carry
+
+        lax.fori_loop(1, coarse, push, 0)
+        keep = pltpu.make_async_copy(buffer.at[gx], in_bodies.at[place], local_sems.at[1 + offset])
+        keep.start()
+        return keep
+
+    kept = [pack(bodies, 0)]
+
+    weights = phase_weights(waves[...])
+    lane = lax.broadcasted_iota(jnp.int32, (KPAD, KPAD), 1)
+    transposed[...] = jnp.zeros_like(transposed)
+
+    def feature_step(pair, carry):
+        for member in range(2):
+            leaf = pair * 2 + member
+            body = pad8(bodies[leaf])
+            basis = basis_leaf(body, weights)
+            harmonic[leaf] = basis
+            column = jnp.sum(lane_fold(basis * body[3:4]), axis=1, keepdims=True)
+            transposed[...] = jnp.where(lane == leaf, column, transposed[...])
+            left[leaf, :, :GROUPS] = left_side(body).T.astype(BF16)
+        return carry
+
+    def near_step(pair, carry):
+        for member in range(4):
+            leaf = pair * 4 + member
+            sides = []
+            for entry in range(2):
+                code = pairs[leaf * 2 + entry]
+                body = pad8(bodies[code & 63])
+                charge = body[3:4] * (code >> 21).astype(F32)
+                sides.append((source_right(body, (code >> 16) & 31), charge))
+            rows = left[leaf][:, :GROUPS]
+            pieces = []
+            for start in range(0, WIDTH, 128):
+                total = sum(pair_rows(rows, side, charge, start, 128) for side, charge in sides)
+                high, low = split2(total)
+                pieces.append(dot_nt(ones, high) + dot_nt(ones, low))
+            near_own[pl.ds(leaf, 1), :] = jnp.concatenate(pieces, axis=1)[:1]
+        return carry
+
+    ones = jnp.ones((8, 128), BF16)
+    left[...] = jnp.zeros_like(left)
+    cuts = (0, 24, 48, 64)
+    lax.fori_loop(cuts[0] // 2, cuts[1] // 2, feature_step, 0)
+
+    first[0].wait_recv()
+    first[1].wait_recv()
+    second = ring(2)
+    kept += [pack(r1, 1), pack(l1, fine - 1)]
+    lax.fori_loop(cuts[1] // 2, cuts[2] // 2, feature_step, 0)
+
+    second[0].wait_recv()
+    second[1].wait_recv()
+    third = ring(3)
+    kept += [pack(r2, 2), pack(l2, fine - 2)]
+    lax.fori_loop(cuts[2] // 2, cuts[3] // 2, feature_step, 0)
+
+    outs = [
+        pltpu.make_async_copy(harmonic, harmonic_out, out_sems.at[0]),
+        pltpu.make_async_copy(left, left_out, out_sems.at[1]),
+    ]
+    for copy in outs:
+        copy.start()
+    own = transposed[...].T[:LEAVES]
+    moments[...] = own
+    column_rows[0, :LEAVES] = own
+    column_rows[0, LEAVES:] = jnp.broadcast_to(upward(own, shift), (8, KPAD))
+    for k in range(1, fine):
+        remote(column_rows.at[0], column_rows.at[k], small_send.at[1], small_recv.at[1],
+               {"gy": lax.rem(gy + k, fine)})
+
+    third[0].wait_recv()
+    third[1].wait_recv()
+    fourth = ring(4)
+    kept += [pack(r3, 3), pack(l3, fine - 3)]
+    lax.fori_loop(0, half // 4, near_step, 0)
+
+    fourth[0].wait_recv()
+    fourth[1].wait_recv()
+    kept += [pack(opposite, fine // 2)]
+
+    others = column_rows.at[pl.ds(1, fine - 1)]
+    pltpu.make_async_copy(others, others, small_recv.at[1]).wait()
+    for offset in range(fine):
+        there = lax.rem(gy + fine - offset, fine)
+
+        def pick(peer, carry):
+            for slot in range(2):
+                row = table_words[offset, 0, peer * 2 + slot]
+                row_pack[peer, pl.ds(there * 2 + slot, 1), :] = column_rows[offset, pl.ds(row, 1), :]
+            row_pack[peer, pl.ds(2 * fine + there, 1), :] = column_rows[offset, LEAVES : LEAVES + 1, :]
+            return carry
+
+        lax.fori_loop(0, coarse, pick, 0)
+
+    def push_rows(j, carry):
+        peer = lax.rem(gx + j, coarse)
+        remote(row_pack.at[peer], in_rows.at[gx], plane_send.at[1], plane_recv.at[1], {"gx": peer})
+        return carry
+
+    lax.fori_loop(1, coarse, push_rows, 0)
+    keep = pltpu.make_async_copy(row_pack.at[gx], in_rows.at[gx], local_sems.at[0])
+    keep.start()
+    kept.append(keep)
+
+    lax.fori_loop(half // 4, LEAVES // 4, near_step, 0)
+
+    for copy in kept + outs:
+        copy.wait()
+    for copy in first + second + third + fourth:
+        copy.wait_send()
+    sent_tables = tables.at[pl.ds(1, fine - 1)]
+    pltpu.make_async_copy(sent_tables, sent_tables, small_send.at[0]).wait()
+    pltpu.make_async_copy(others, others, small_send.at[1]).wait()
+    sent = in_bodies.at[pl.ds(0, (coarse - 1) * fine * 2)]
+    pltpu.make_async_copy(sent, sent, plane_send.at[0]).wait()
+    pltpu.make_async_copy(sent, sent, plane_recv.at[0]).wait()
+    sent = in_rows.at[pl.ds(0, coarse - 1)]
+    pltpu.make_async_copy(sent, sent, plane_send.at[1]).wait()
+    pltpu.make_async_copy(sent, sent, plane_recv.at[1]).wait()
+
+
+def run_exchange(pairs, bodies, table, waves, shift, coarse, fine):
+    block = pltpu.VMEM((LEAVES, 4, WIDTH), F32)
+    return pl.pallas_call(
+        exchange_kernel,
+        out_shape=[
+            jax.ShapeDtypeStruct((coarse * fine * 2, 4, WIDTH), F32),
+            jax.ShapeDtypeStruct((coarse, 3 * fine, KPAD), F32),
+            jax.ShapeDtypeStruct((LEAVES, KPAD, WIDTH), F32),
+            jax.ShapeDtypeStruct((LEAVES, WIDTH, 128), BF16),
+            jax.ShapeDtypeStruct((LEAVES, KPAD), F32),
+            jax.ShapeDtypeStruct((LEAVES, WIDTH), F32),
+        ],
+        in_specs=[SMEM] + [VMEM] * 4,
+        out_specs=[ANY] * 4 + [VMEM] * 2,
+        scratch_shapes=[block] * 7
+        + [
+            pltpu.VMEM((fine, coarse, 2, 4, WIDTH), F32),
+            pltpu.VMEM((LEAVES, KPAD, WIDTH), F32),
+            pltpu.VMEM((LEAVES, WIDTH, 128), BF16),
+            pltpu.VMEM((KPAD, KPAD), F32),
+            pltpu.VMEM((fine, LEAVES + 8, KPAD), F32),
+            pltpu.VMEM((coarse, 3 * fine, KPAD), F32),
+            pltpu.VMEM((fine, 8, 128), jnp.int32),
+            pltpu.SMEM((fine, 8, 128), jnp.int32),
+            pltpu.SemaphoreType.DMA((8,)),
+            pltpu.SemaphoreType.DMA((8,)),
+            pltpu.SemaphoreType.DMA((2,)),
+            pltpu.SemaphoreType.DMA((2,)),
+            pltpu.SemaphoreType.DMA((2,)),
+            pltpu.SemaphoreType.DMA((2,)),
+            pltpu.SemaphoreType.DMA((1 + fine,)),
+            pltpu.SemaphoreType.DMA((2,)),
+        ],
+        compiler_params=pltpu.CompilerParams(
+            vmem_limit_bytes=60 << 20, collective_id=0, has_side_effects=True
+        ),
+        cost_estimate=pl.CostEstimate(flops=40_000_000_000, bytes_accessed=40_000_000, transcendentals=0),
+    )(pairs, bodies, table, waves, shift)
 
 
 def local(
@@ -349,35 +553,38 @@
 ):
     leaves = far_src.shape[0]
     peers, slot_count = send_leaf.shape[1:]
-    coarse_size = lax.axis_size("gx")
-    fine_size = lax.axis_size("gy")
+    coarse = lax.axis_size("gx")
+    fine = lax.axis_size("gy")
     bodies = (
         jnp.concatenate([positions, charges[None, :]], axis=0)
         .reshape(4, leaves, WIDTH)
         .transpose(1, 0, 2)
     )
-    chosen = send_leaf[0]
-    in_bodies = exchange(
-        bodies[chosen].reshape(coarse_size, fine_size, slot_count, 4, WIDTH)
-    ).reshape(peers * slot_count, 4, WIDTH)
+    table = send_leaf[0].reshape(coarse, fine, slot_count).transpose(1, 0, 2)
+    table = jnp.pad(
+        table.reshape(fine, 1, coarse * slot_count),
+        ((0, 0), (0, 7), (0, 128 - coarse * slot_count)),
+    )
+    column = jnp.arange(near_src.shape[1], dtype=jnp.int32)[None, :]
+    own = (near_src >= 0) & (near_src < leaves) & (column > 0)
+    first_own = jnp.min(jnp.where(own, column, near_src.shape[1]), axis=1, keepdims=True)
+    taken = column == first_own
+    word = near_src + near_shift * 65536 + (1 << 21)
+    pairs = jnp.stack(
+        [word[:, 0], jnp.sum(jnp.where(taken, word, 0), axis=1)], axis=1
+    ).reshape(-1)
     waves = wave_rows(moment_freq, moment_phase)
     shift = pad_ops(child_parent_shift_matrix)
-    m2l = pad_ops(m2l_ops)
-    harmonic, left, moments, top = run_features(bodies, waves, shift)
-    sent = jnp.concatenate(
-        [moments[chosen], jnp.broadcast_to(top[:1][None], (peers, 1, KPAD))], axis=1
-    )
-    came = exchange(sent.reshape(coarse_size, fine_size, slot_count + 1, KPAD)).reshape(
-        peers, slot_count + 1, KPAD
-    )
-    in_moments = came[:, :slot_count].reshape(peers * slot_count, KPAD)
-    tops = came[:, slot_count]
-    codes, count = near_codes(near_src, near_shift, near_src >= 0)
+    in_bodies, in_rows, harmonic, left, moments, near_own = run_exchange(
+        pairs, bodies, table, waves, shift, coarse, fine
+    )
+    wanted = (near_src >= 0) & (column > 0) & ~taken
+    codes, count = near_codes(near_src, near_shift, wanted)
     rows = leaves + peers * slot_count + 32
     far_index = jnp.where(far_src >= 0, far_class * rows + far_src, 16 * rows).reshape(-1)
     result = run_finish(
-        count, codes, far_index, top_list[0], top_class[0], left, m2l, shift,
-        moments, in_moments, tops, harmonic, bodies, in_bodies,
+        count, codes, far_index, top_list[0], top_class[0], left, pad_ops(m2l_ops), shift,
+        moments, in_rows, near_own, harmonic, bodies, in_bodies,
     )
     return result.reshape(leaves * WIDTH)
 

time: 320 us -> 205 us (0.64)
  waiting for transfers between devices: 151 us -> 0 us
  Pallas kernels: 103 us -> 186 us
  starting transfers between devices: 27.6 us -> 0 us
  local copies, waits for them, and re-layouts: 28.3 us -> 9.86 us
    all_to_all x4 -> x0, waiting for transfers between devices: 151 us -> none  [the longest x2 100 us: exchange(): return lax.all_to_all(values, 'gy', split_axis=1, concat_axis=1, tiled=True)]
    pallas_call x1, Pallas kernels: 28.8 us -> 130 us  [run_exchange(): pl.pallas_call(exchange_kernel, out_shape=[jax.ShapeDtypeStruct((coarse *...]
    all_to_all x4 -> x0, starting transfers between devices: 27.6 us -> none  [the longest x2 14.5 us: exchange(): lax.all_to_all(values, 'gx', split_axis=0, concat_axis=0, tiled=True)]
    pallas_call x1, Pallas kernels: 73.9 us -> 56.1 us  [run_finish(): pl.pallas_call(finish_kernel, out_shape=jax.ShapeDtypeStruct((LEAVES, WID...]
    all_to_all x4 -> x0, local copies, waits for them, and re-layouts: 12.1 us -> none  [the longest x2 6.33 us: exchange(): lax.all_to_all(values, 'gx', split_axis=0, concat_axis=0, tiled=True)]
    gather x3 -> x0, local copies, waits for them, and re-layouts: 6.45 us -> none  [the longest x1 4.65 us: local(): bodies[chosen].reshape(coarse_size, fine_size, slot_count, 4, WIDTH)]
  transfers between devices with their start and end apart: 4 -> 0, of which waited for: 4 -> 0; matrix products, arithmetic and copies ran while one was open for 5% -> 0% of each run, Pallas kernels for 0% -> 0%
where the time goes in v2:
time: 205 us; the launch traced here: 204 us
  Pallas kernels  186 us (91%)
  local copies, waits for them, and re-layouts  9.86 us (5%)
  other arithmetic  8.04 us (4%)
    pallas_call x1, Pallas kernels, run_exchange(): pl.pallas_call(exchange_kernel, out_shape=[jax.ShapeDtypeStruct((coarse *...  130 us
    pallas_call x1, Pallas kernels, run_finish(): pl.pallas_call(finish_kernel, out_shape=jax.ShapeDtypeStruct((LEAVES, WID...  56.1 us
    unnamed x3, local copies, waits for them, and re-layouts  4.25 us

profile of v2, /device:TPU:6, one launch (start us, length us, event | category | flops | bytes accessed | tf_op | source)
XLA Modules:
  0.0 204.2 jit_solution(16276381586012793200)
XLA Ops:
  0.0 0.8 select_reduce_fusion.2
  0.8 0.7 multiply_bitcast_fusion
  1.4 1.3 select_maximum_fusion.waves
  2.7 1.5 select_reduce_fusion.1
  4.2 0.1 copy.27
  4.3 0.1 reshape.66
  4.4 0.2 convert_reduce_fusion
  4.6 0.7 add_select_fusion
  5.3 0.1 copy.30
  5.4 0.7 reshape.67.far_index
  6.1 0.1 copy.31
  6.2 0.7 reshape.68.pairs
  6.9 0.1 copy.29
  7.0 0.1 mul.45
  7.1 0.1 copy.28
  7.2 0.1 mul.42
  7.3 0.8 select_reduce_fusion.codes
  8.0 0.8 reshape_squeeze.3
  8.8 0.1 copy.33
  8.9 0.6 pad.16.table
  9.5 2.1 %maximum_bitcast_fusion.bodies.bodies_hbm = f32[64,4,512]{2,1,0:T(4,128)} fusion(f32[1,64,512]{2,0,1:T(1,128)} %bitcast.17, f32[3,64,512]{2,0,1:T(4,128)} %bitcast.16), kind=kLoop, calls=%fused_computation.5 | loop fusion | flops 131072 | bytes 1048576 | tf_op jit(solution)/shard_map/transpose | solution.py:561
  11.7 1.1 copy.34
  12.8 0.8 pad.18.shift
  13.7 1.5 copy.35
  15.2 1.2 pad.19.m2l
  16.3 130.1 %shard_map.127 = (f32[512,4,512]{2,1,0:T(4,128)}, f32[32,24,128]{2,1,0:T(8,128)}, f32[64,128,512]{2,1,0:T(8,128)}, bf16[64,512,128]{2,1,0:T(8,128)(2,1)}, f32[64,128]{1,0:T(8,128)}, /*index=5*/f32[64,512]{1,0:T(8,128)}) custom-call(s32[128]{0:T(128)} %reshape.68.pairs, f32[64,4,512]{2,1,0:T(4,128)} %maximum_bitcast_fusion.bodies.bodies_hbm, ...), custom_call_target="tpu_custom_call" | custom-call | flops 40000000000 | bytes 40000000 | tf_op jit(solution)/shard_map/pallas_call | solution.py:500
  146.5 56.1 %shard_map.128 = f32[64,512]{1,0:T(8,128)} custom-call(s32[1]{0:T(128)} %bitcast.count, s32[512]{0:T(512)} %select_reduce_fusion.codes, s32[2048]{0:T(1024)} %reshape.67.far_index, s32[32]{0:T(128)} %bitcast.22, s32[32]{0:T(128)} %bitcast.23, bf16[64,512,128]{2,1,0:T(8,128)(2,1)} %get-tuple-element.11.left, f32[16,128,128]{2,1,0:T(8,128)} %pad.19.m2l, ...), custom_call_target="tpu_custom_call" | custom-call | flops 60000002048 | bytes 40000000 | tf_op jit(solution)/shard_map/pallas_call | solution.py:277
  202.6 1.6 copy.36
  (5 shorter events, 0.1 us)

commit v3 on v2

--- a/solution.py
+++ b/solution.py
@@ -146,6 +146,48 @@
     return lane_fold(value)
 
 
+def near_fields(near_src, near_shift):
+    source = near_src[...]
+    column = lax.broadcasted_iota(jnp.int32, source.shape, 0)
+    own = (source >= 0) & (source < LEAVES) & (column > 0)
+    first_own = jnp.min(jnp.where(own, column.astype(F32), 8.0), axis=0, keepdims=True)
+    taken = column.astype(F32) == first_own
+    wanted = (source >= 0) & (column > 0) & jnp.logical_not(taken)
+    word = (source + near_shift[...] * 65536 + (1 << 21)).astype(F32)
+    return word, taken, wanted, source
+
+
+def near_list(near_src, near_shift, listed):
+    word, _, wanted, source = near_fields(near_src, near_shift)
+    word = word + (source * 63 + lax.broadcasted_iota(jnp.int32, source.shape, 1)).astype(F32)
+    mark = jnp.where(wanted, 1.0, 0.0)
+    before = lax.broadcasted_iota(jnp.int32, (LEAVES, LEAVES), 0)
+    before = before < lax.broadcasted_iota(jnp.int32, (LEAVES, LEAVES), 1)
+    place = dot_nn(mark.astype(BF16), jnp.where(before, 1.0, 0.0).astype(BF16))
+    totals = jnp.sum(mark, axis=1, keepdims=True)
+    row = lax.broadcasted_iota(jnp.int32, (8, LEAVES), 0)
+    for column in range(8):
+        place = place + jnp.where(row > column, totals[column : column + 1], 0.0)
+    place = jnp.where(wanted, place, -1.0).astype(jnp.int32)
+    parts = split3(word)
+    low_row = lax.broadcasted_iota(jnp.int32, (LEAVES, LEAVES), 0)
+    codes = jnp.zeros((8, LEAVES), F32)
+    for column in range(8):
+        at = place[column : column + 1]
+        low = jnp.where(low_row == (at & 63), 1.0, 0.0).astype(BF16)
+        for part in parts:
+            high = jnp.where(row == (at >> 6), part[column : column + 1], 0.0).astype(BF16)
+            codes = codes + dot_nt(high, low)
+    number = jnp.broadcast_to(jnp.sum(totals, axis=0, keepdims=True), (8, 128))
+    listed[...] = number.astype(jnp.int32)
+    listed[:, :LEAVES] = codes.astype(jnp.int32)
+
+
+def pad_into(padded, ops):
+    padded[...] = jnp.zeros_like(padded)
+    padded[:, : ops.shape[1], : ops.shape[2]] = ops[...]
+
+
 def local_expansions(pool_moments, m2l, shift, table, far_index, top_class, expansions):
     rows = pool_moments.shape[0]
     pool_high, pool_low = split2(pool_moments[...])
@@ -162,7 +204,7 @@
         return parts[0]
 
     top_local = tree(
-        [table[pl.ds(top_class[e] * rows + (rows - 32 + e), 1), :] for e in range(32)]
+        [table[pl.ds(top_class[0, e] * rows + (rows - 32 + e), 1), :] for e in range(32)]
     )
     top_rows = jnp.broadcast_to(top_local, (8, KPAD))
     row = lax.broadcasted_iota(jnp.int32, (8, KPAD), 0)
@@ -171,9 +213,8 @@
         down = jnp.where(row == child, dot3(dot_nn, top_rows, shift[child]), down)
 
     def gather(leaf, carry):
-        base = leaf * 32
         expansions[pl.ds(leaf, 1), :] = tree(
-            [table[pl.ds(far_index[base + e], 1), :] for e in range(32)]
+            [table[pl.ds(far_index[e, leaf], 1), :] for e in range(32)]
         )
         return carry
 
@@ -182,20 +223,43 @@
 
 
 def finish_kernel(
-    count, codes, far_index, top_list, top_class,
-    left, m2l, shift, own_moments, in_rows, near_own,
-    harmonic_hbm, bodies_hbm, in_bodies_hbm,
+    top_list, top_class,
+    near_src, near_shift, far_src, far_class, m2l_ops, shift_ops, own_moments, in_rows,
+    left_hbm, near_hbm, harmonic_hbm, bodies_hbm, in_bodies_hbm,
     out,
-    pool, harmonic, near, pool_moments, table, expansions, sems,
+    pool, left, near, harmonic, pool_moments, table, expansions, m2l, shift,
+    listed, far_rows, codes, far_index, sems,
 ):
     slots = in_bodies_hbm.shape[0]
-    copy_own = pltpu.make_async_copy(bodies_hbm, pool.at[pl.ds(0, LEAVES)], sems.at[0])
-    copy_in = pltpu.make_async_copy(in_bodies_hbm, pool.at[pl.ds(LEAVES, slots)], sems.at[1])
-    copy_harmonic = pltpu.make_async_copy(harmonic_hbm, harmonic, sems.at[2])
-    copy_own.start()
-    copy_in.start()
-    copy_harmonic.start()
-    near[...] = jnp.zeros_like(near)
+    copies = [
+        pltpu.make_async_copy(source, target, sems.at[place])
+        for place, (source, target) in enumerate(
+            (
+                (left_hbm, left),
+                (bodies_hbm, pool.at[pl.ds(0, LEAVES)]),
+                (in_bodies_hbm, pool.at[pl.ds(LEAVES, slots)]),
+                (near_hbm, near),
+                (harmonic_hbm, harmonic),
+            )
+        )
+    ]
+    for copy in copies:
+        copy.start()
+    entry_rows = 16 * (LEAVES + slots + 32)
+    source = far_src[...]
+    far_rows[...] = jnp.zeros_like(far_rows)
+    far_rows[:, :LEAVES] = jnp.where(
+        source >= 0, far_class[...] * (entry_rows // 16) + source, entry_rows
+    )
+    near_list(near_src, near_shift, listed)
+    words = [
+        pltpu.make_async_copy(far_rows, far_index, sems.at[5]),
+        pltpu.make_async_copy(listed, codes, sems.at[6]),
+    ]
+    for copy in words:
+        copy.start()
+    pad_into(m2l, m2l_ops)
+    pad_into(shift, shift_ops)
     rows = LEAVES + slots
     pool_moments[:LEAVES] = own_moments[...]
     fine = in_rows.shape[1] // 3
@@ -203,19 +267,21 @@
         start = LEAVES + 2 * fine * peer
         pool_moments[start : start + 2 * fine] = in_rows[peer, : 2 * fine]
     for e in range(32):
-        owner = top_list[e]
+        owner = top_list[0, e]
         pool_moments[rows + e : rows + e + 1, :] = in_rows[
             owner // fine, pl.ds(2 * fine + lax.rem(owner, fine), 1), :
         ]
+    for copy in words:
+        copy.wait()
     local = local_expansions(pool_moments, m2l, shift, table, far_index, top_class, expansions)
     local_columns = jnp.concatenate([local, jnp.zeros((KPAD - LEAVES, KPAD), F32)], axis=0).T
 
-    copy_own.wait()
-    copy_in.wait()
+    for copy in copies[:4]:
+        copy.wait()
 
     def near_step(group, carry):
         for member in range(UNROLL):
-            code = codes[group * UNROLL + member]
+            code = codes[group >> 3, (group & 7) * UNROLL + member]
             target = code & 63
             source = (code >> 6) & 1023
             live = (code >> 21).astype(F32)
@@ -228,8 +294,8 @@
                 )
         return carry
 
-    lax.fori_loop(0, (count[0] + UNROLL - 1) // UNROLL, near_step, 0)
-    copy_harmonic.wait()
+    lax.fori_loop(0, (codes[0, LEAVES] + UNROLL - 1) // UNROLL, near_step, 0)
+    copies[4].wait()
     ones = jnp.ones((8, 128), BF16)
 
     def far_step(group, columns):
@@ -239,22 +305,10 @@
             far = jnp.sum(product, axis=0, keepdims=True)
             near_high, near_low = split2(near[leaf])
             total = dot_nt(ones, near_high) + dot_nt(ones, near_low)
-            out[pl.ds(leaf, 1), :] = total[:1] + far + near_own[pl.ds(leaf, 1), :]
+            out[leaf] = total[:1] + far
         return pltpu.roll(columns, KPAD - 8, 1)
 
     lax.fori_loop(0, LEAVES // 8, far_step, local_columns)
-
-
-def near_codes(near_src, near_shift, wanted):
-    number = near_src.size
-    flat = near_src.reshape(number)
-    entry = jnp.arange(number, dtype=jnp.int32)
-    code = (entry // near_src.shape[1]) + flat * 64 + near_shift.reshape(number) * 65536 + (1 << 21)
-    wanted = wanted.reshape(number)
-    place = jnp.sum(wanted[None, :] & (entry[None, :] < entry[:, None]), axis=1, dtype=jnp.int32)
-    place = jnp.where(wanted, place, -1)
-    codes = jnp.sum(jnp.where(place[None, :] == entry[:, None], code[None, :], 0), axis=1)
-    return codes, jnp.sum(wanted, dtype=jnp.int32)[None]
 
 
 SMEM = pl.BlockSpec(memory_space=pltpu.SMEM)
@@ -262,42 +316,47 @@
 ANY = pl.BlockSpec(memory_space=pl.ANY)
 
 
-def pad_ops(ops):
-    return jnp.pad(ops, ((0, 0), (0, KPAD - ops.shape[1]), (0, KPAD - ops.shape[2])))
-
-
-def wave_rows(moment_freq, moment_phase):
-    rows = jnp.concatenate([moment_freq, moment_phase[None] * (0.5 / math.pi)], axis=0)
-    return jnp.pad(rows, ((0, 0), (0, KPAD - rows.shape[1])))
-
-
-def run_finish(count, codes, far_index, top_list, top_class, left, m2l, shift, moments, in_rows, near_own, harmonic, bodies, in_bodies):
+def run_finish(
+    top_list, top_class, near_src, near_shift, far_src, far_class, m2l, shift, moments, in_rows,
+    left, near, harmonic, bodies, in_bodies,
+):
     slots = in_bodies.shape[0]
     rows = LEAVES + slots + 32
     return pl.pallas_call(
         finish_kernel,
-        out_shape=jax.ShapeDtypeStruct((LEAVES, WIDTH), F32),
-        in_specs=[SMEM] * 5 + [VMEM] * 6 + [ANY] * 3,
+        out_shape=jax.ShapeDtypeStruct((LEAVES, 1, WIDTH), F32),
+        in_specs=[SMEM] * 2 + [VMEM] * 8 + [ANY] * 5,
         out_specs=VMEM,
         scratch_shapes=[
             pltpu.VMEM((LEAVES + slots, 4, WIDTH), F32),
+            pltpu.VMEM((LEAVES, WIDTH, 128), BF16),
+            pltpu.VMEM((LEAVES, WIDTH, 128), F32),
             pltpu.VMEM((LEAVES, KPAD, WIDTH), F32),
-            pltpu.VMEM((LEAVES, WIDTH, 128), F32),
             pltpu.VMEM((rows, KPAD), F32),
             pltpu.VMEM((16 * rows + 8, KPAD), F32),
             pltpu.VMEM((LEAVES, KPAD), F32),
-            pltpu.SemaphoreType.DMA((3,)),
+            pltpu.VMEM((16, KPAD, KPAD), F32),
+            pltpu.VMEM((8, KPAD, KPAD), F32),
+            pltpu.VMEM((8, 128), jnp.int32),
+            pltpu.VMEM((32, 128), jnp.int32),
+            pltpu.SMEM((8, 128), jnp.int32),
+            pltpu.SMEM((32, 128), jnp.int32),
+            pltpu.SemaphoreType.DMA((7,)),
         ],
         compiler_params=pltpu.CompilerParams(vmem_limit_bytes=62 << 20),
         cost_estimate=pl.CostEstimate(flops=60_000_000_000, bytes_accessed=40_000_000, transcendentals=0),
-    )(count, codes, far_index, top_list, top_class, left, m2l, shift, moments, in_rows, near_own, harmonic, bodies, in_bodies)
+    )(
+        top_list, top_class, near_src, near_shift, far_src, far_class, m2l, shift, moments, in_rows,
+        left, near, harmonic, bodies, in_bodies,
+    )
 
 
 def exchange_kernel(
-    pairs, bodies, table, waves, shift,
-    in_bodies, in_rows, harmonic_out, left_out, moments, near_own,
+    positions, charges, send_table, near_src, near_shift, freq, phase, shift_ops,
+    in_bodies, in_rows, harmonic_out, left_out, near_out, moments, bodies,
     r1, r2, r3, l1, l2, l3, opposite,
-    packs, harmonic, left, transposed, column_rows, row_pack, tables, table_words,
+    packs, harmonic, left, near, shift, waves, transposed, column_rows, row_pack,
+    table, tables, table_words, pair_words, pairs,
     ring_send, ring_recv, small_send, small_recv, plane_send, plane_recv, local_sems, out_sems,
 ):
     gx, gy = lax.axis_index("gx"), lax.axis_index("gy")
@@ -306,6 +365,16 @@
     back = {"gy": lax.rem(gy + fine - 1, fine)}
     half = LEAVES // 2
 
+    def build(quad, carry):
+        for member in range(4):
+            leaf = quad * 4 + member
+            place = pl.ds(pl.multiple_of(leaf * WIDTH, WIDTH), WIDTH)
+            bodies[leaf] = jnp.concatenate([positions[:, place], charges[leaf]], axis=0)
+        return carry
+
+    lax.fori_loop(0, LEAVES // 4, build, 0)
+    table[...] = jnp.zeros_like(table)
+    table[: send_table.shape[0], :] = send_table[...]
     barrier = pltpu.get_barrier_semaphore()
 
     def greet_plane(j, carry):
@@ -343,8 +412,8 @@
     first = ring(1)
     for k in range(1, fine):
         there = lax.rem(gy + k, fine)
-        remote(table.at[there], tables.at[k], small_send.at[0], small_recv.at[0], {"gy": there})
-    own_table = pltpu.make_async_copy(table.at[gy], tables.at[0], local_sems.at[0])
+        remote(table, tables.at[k], small_send.at[0], small_recv.at[0], {"gy": there})
+    own_table = pltpu.make_async_copy(table, tables.at[0], local_sems.at[0])
     own_table.start()
     own_table.wait()
     others = tables.at[pl.ds(1, fine - 1)]
@@ -362,7 +431,7 @@
             for part in range(4):
                 peer = quad * 4 + part
                 for slot in range(2):
-                    buffer[peer, slot] = block[table_words[offset, 0, peer * 2 + slot]]
+                    buffer[peer, slot] = block[table_words[offset, slot, peer * fine + gy]]
             return carry
 
         lax.fori_loop(0, coarse // 4, one, 0)
@@ -380,13 +449,26 @@
 
     kept = [pack(bodies, 0)]
 
+    word, taken, _, _ = near_fields(near_src, near_shift)
+    pair_words[...] = jnp.zeros_like(pair_words)
+    pair_words[:1, :LEAVES] = word[:1].astype(jnp.int32)
+    pair_words[1:2, :LEAVES] = jnp.sum(
+        jnp.where(taken, word, 0.0), axis=0, keepdims=True
+    ).astype(jnp.int32)
+    words = pltpu.make_async_copy(pair_words, pairs, local_sems.at[0])
+    words.start()
+    words.wait()
+    pad_into(shift, shift_ops)
+    waves[...] = jnp.zeros_like(waves)
+    waves[:3, : freq.shape[1]] = freq[...]
+    waves[3:4, : freq.shape[1]] = phase[...] * (0.5 / math.pi)
     weights = phase_weights(waves[...])
     lane = lax.broadcasted_iota(jnp.int32, (KPAD, KPAD), 1)
     transposed[...] = jnp.zeros_like(transposed)
 
-    def feature_step(pair, carry):
-        for member in range(2):
-            leaf = pair * 2 + member
+    def feature_step(quad, carry):
+        for member in range(4):
+            leaf = quad * 4 + member
             body = pad8(bodies[leaf])
             basis = basis_leaf(body, weights)
             harmonic[leaf] = basis
@@ -395,40 +477,37 @@
             left[leaf, :, :GROUPS] = left_side(body).T.astype(BF16)
         return carry
 
-    def near_step(pair, carry):
+    def near_step(quad, carry):
         for member in range(4):
-            leaf = pair * 4 + member
+            leaf = quad * 4 + member
             sides = []
             for entry in range(2):
-                code = pairs[leaf * 2 + entry]
+                code = pairs[entry, leaf]
                 body = pad8(bodies[code & 63])
                 charge = body[3:4] * (code >> 21).astype(F32)
                 sides.append((source_right(body, (code >> 16) & 31), charge))
             rows = left[leaf][:, :GROUPS]
-            pieces = []
             for start in range(0, WIDTH, 128):
-                total = sum(pair_rows(rows, side, charge, start, 128) for side, charge in sides)
-                high, low = split2(total)
-                pieces.append(dot_nt(ones, high) + dot_nt(ones, low))
-            near_own[pl.ds(leaf, 1), :] = jnp.concatenate(pieces, axis=1)[:1]
+                near[leaf, start : start + 128] = sum(
+                    pair_rows(rows, side, charge, start, 128) for side, charge in sides
+                )
         return carry
 
-    ones = jnp.ones((8, 128), BF16)
     left[...] = jnp.zeros_like(left)
     cuts = (0, 24, 48, 64)
-    lax.fori_loop(cuts[0] // 2, cuts[1] // 2, feature_step, 0)
+    lax.fori_loop(cuts[0] // 4, cuts[1] // 4, feature_step, 0)
 
     first[0].wait_recv()
     first[1].wait_recv()
     second = ring(2)
     kept += [pack(r1, 1), pack(l1, fine - 1)]
-    lax.fori_loop(cuts[1] // 2, cuts[2] // 2, feature_step, 0)
+    lax.fori_loop(cuts[1] // 4, cuts[2] // 4, feature_step, 0)
 
     second[0].wait_recv()
     second[1].wait_recv()
     third = ring(3)
     kept += [pack(r2, 2), pack(l2, fine - 2)]
-    lax.fori_loop(cuts[2] // 2, cuts[3] // 2, feature_step, 0)
+    lax.fori_loop(cuts[2] // 4, cuts[3] // 4, feature_step, 0)
 
     outs = [
         pltpu.make_async_copy(harmonic, harmonic_out, out_sems.at[0]),
@@ -449,6 +528,10 @@
     fourth = ring(4)
     kept += [pack(r3, 3), pack(l3, fine - 3)]
     lax.fori_loop(0, half // 4, near_step, 0)
+    outs.append(
+        pltpu.make_async_copy(near.at[pl.ds(0, half)], near_out.at[pl.ds(0, half)], out_sems.at[2])
+    )
+    outs[-1].start()
 
     fourth[0].wait_recv()
     fourth[1].wait_recv()
@@ -459,14 +542,20 @@
     for offset in range(fine):
         there = lax.rem(gy + fine - offset, fine)
 
-        def pick(peer, carry):
-            for slot in range(2):
-                row = table_words[offset, 0, peer * 2 + slot]
-                row_pack[peer, pl.ds(there * 2 + slot, 1), :] = column_rows[offset, pl.ds(row, 1), :]
-            row_pack[peer, pl.ds(2 * fine + there, 1), :] = column_rows[offset, LEAVES : LEAVES + 1, :]
+        def pick(quad, carry):
+            for part in range(4):
+                peer = quad * 4 + part
+                for slot in range(2):
+                    row = table_words[offset, slot, peer * fine + gy]
+                    row_pack[peer, pl.ds(there * 2 + slot, 1), :] = column_rows[
+                        offset, pl.ds(row, 1), :
+                    ]
+                row_pack[peer, pl.ds(2 * fine + there, 1), :] = column_rows[
+                    offset, LEAVES : LEAVES + 1, :
+                ]
             return carry
 
-        lax.fori_loop(0, coarse, pick, 0)
+        lax.fori_loop(0, coarse // 4, pick, 0)
 
     def push_rows(j, carry):
         peer = lax.rem(gx + j, coarse)
@@ -479,6 +568,12 @@
     kept.append(keep)
 
     lax.fori_loop(half // 4, LEAVES // 4, near_step, 0)
+    outs.append(
+        pltpu.make_async_copy(
+            near.at[pl.ds(half, half)], near_out.at[pl.ds(half, half)], out_sems.at[3]
+        )
+    )
+    outs[-1].start()
 
     for copy in kept + outs:
         copy.wait()
@@ -495,7 +590,7 @@
     pltpu.make_async_copy(sent, sent, plane_recv.at[1]).wait()
 
 
-def run_exchange(pairs, bodies, table, waves, shift, coarse, fine):
+def run_exchange(positions, charges, send_table, near_src, near_shift, freq, phase, shift, coarse, fine):
     block = pltpu.VMEM((LEAVES, 4, WIDTH), F32)
     return pl.pallas_call(
         exchange_kernel,
@@ -504,21 +599,28 @@
             jax.ShapeDtypeStruct((coarse, 3 * fine, KPAD), F32),
             jax.ShapeDtypeStruct((LEAVES, KPAD, WIDTH), F32),
             jax.ShapeDtypeStruct((LEAVES, WIDTH, 128), BF16),
+            jax.ShapeDtypeStruct((LEAVES, WIDTH, 128), F32),
             jax.ShapeDtypeStruct((LEAVES, KPAD), F32),
-            jax.ShapeDtypeStruct((LEAVES, WIDTH), F32),
+            jax.ShapeDtypeStruct((LEAVES, 4, WIDTH), F32),
         ],
-        in_specs=[SMEM] + [VMEM] * 4,
-        out_specs=[ANY] * 4 + [VMEM] * 2,
+        in_specs=[VMEM] * 8,
+        out_specs=[ANY] * 5 + [VMEM] * 2,
         scratch_shapes=[block] * 7
         + [
             pltpu.VMEM((fine, coarse, 2, 4, WIDTH), F32),
             pltpu.VMEM((LEAVES, KPAD, WIDTH), F32),
             pltpu.VMEM((LEAVES, WIDTH, 128), BF16),
+            pltpu.VMEM((LEAVES, WIDTH, 128), F32),
+            pltpu.VMEM((8, KPAD, KPAD), F32),
+            pltpu.VMEM((4, KPAD), F32),
             pltpu.VMEM((KPAD, KPAD), F32),
             pltpu.VMEM((fine, LEAVES + 8, KPAD), F32),
             pltpu.VMEM((coarse, 3 * fine, KPAD), F32),
-            pltpu.VMEM((fine, 8, 128), jnp.int32),
-            pltpu.SMEM((fine, 8, 128), jnp.int32),
+            pltpu.VMEM((8, coarse * fine), jnp.int32),
+            pltpu.VMEM((fine, 8, coarse * fine), jnp.int32),
+            pltpu.SMEM((fine, 8, coarse * fine), jnp.int32),
+            pltpu.VMEM((8, 128), jnp.int32),
+            pltpu.SMEM((8, 128), jnp.int32),
             pltpu.SemaphoreType.DMA((8,)),
             pltpu.SemaphoreType.DMA((8,)),
             pltpu.SemaphoreType.DMA((2,)),
@@ -526,13 +628,13 @@
             pltpu.SemaphoreType.DMA((2,)),
             pltpu.SemaphoreType.DMA((2,)),
             pltpu.SemaphoreType.DMA((1 + fine,)),
-            pltpu.SemaphoreType.DMA((2,)),
+            pltpu.SemaphoreType.DMA((4,)),
         ],
         compiler_params=pltpu.CompilerParams(
-            vmem_limit_bytes=60 << 20, collective_id=0, has_side_effects=True
+            vmem_limit_bytes=62 << 20, collective_id=0, has_side_effects=True
         ),
-        cost_estimate=pl.CostEstimate(flops=40_000_000_000, bytes_accessed=40_000_000, transcendentals=0),
-    )(pairs, bodies, table, waves, shift)
+        cost_estimate=pl.CostEstimate(flops=40_000_000_000, bytes_accessed=60_000_000, transcendentals=0),
+    )(positions, charges, send_table, near_src, near_shift, freq, phase, shift)
 
 
 def local(
@@ -552,39 +654,22 @@
     top_class,
 ):
     leaves = far_src.shape[0]
-    peers, slot_count = send_leaf.shape[1:]
-    coarse = lax.axis_size("gx")
-    fine = lax.axis_size("gy")
-    bodies = (
-        jnp.concatenate([positions, charges[None, :]], axis=0)
-        .reshape(4, leaves, WIDTH)
-        .transpose(1, 0, 2)
-    )
-    table = send_leaf[0].reshape(coarse, fine, slot_count).transpose(1, 0, 2)
-    table = jnp.pad(
-        table.reshape(fine, 1, coarse * slot_count),
-        ((0, 0), (0, 7), (0, 128 - coarse * slot_count)),
-    )
-    column = jnp.arange(near_src.shape[1], dtype=jnp.int32)[None, :]
-    own = (near_src >= 0) & (near_src < leaves) & (column > 0)
-    first_own = jnp.min(jnp.where(own, column, near_src.shape[1]), axis=1, keepdims=True)
-    taken = column == first_own
-    word = near_src + near_shift * 65536 + (1 << 21)
-    pairs = jnp.stack(
-        [word[:, 0], jnp.sum(jnp.where(taken, word, 0), axis=1)], axis=1
-    ).reshape(-1)
-    waves = wave_rows(moment_freq, moment_phase)
-    shift = pad_ops(child_parent_shift_matrix)
-    in_bodies, in_rows, harmonic, left, moments, near_own = run_exchange(
-        pairs, bodies, table, waves, shift, coarse, fine
-    )
-    wanted = (near_src >= 0) & (column > 0) & ~taken
-    codes, count = near_codes(near_src, near_shift, wanted)
-    rows = leaves + peers * slot_count + 32
-    far_index = jnp.where(far_src >= 0, far_class * rows + far_src, 16 * rows).reshape(-1)
+    in_bodies, in_rows, harmonic, left, near, moments, bodies = run_exchange(
+        positions,
+        charges.reshape(leaves, 1, WIDTH),
+        send_leaf[0].T,
+        near_src.T,
+        near_shift.T,
+        moment_freq,
+        moment_phase[None],
+        child_parent_shift_matrix,
+        lax.axis_size("gx"),
+        lax.axis_size("gy"),
+    )
     result = run_finish(
-        count, codes, far_index, top_list[0], top_class[0], left, pad_ops(m2l_ops), shift,
-        moments, in_rows, near_own, harmonic, bodies, in_bodies,
+        top_list, top_class, near_src.T, near_shift.T, far_src.T, far_class.T,
+        m2l_ops, child_parent_shift_matrix, moments, in_rows,
+        left, near, harmonic, bodies, in_bodies,
     )
     return result.reshape(leaves * WIDTH)
 

time: 205 us -> 159 us (0.78)
  the two profiles are of different devices: /device:TPU:6 before, /device:TPU:0 now
where the time goes in v3:
time: 159 us; the launch traced here: 158 us
  Pallas kernels  154 us (97%)
  local copies, waits for them, and re-layouts  4.44 us (3%)
    pallas_call x1, Pallas kernels, run_exchange(): pl.pallas_call(exchange_kernel, out_shape=[jax.ShapeDtypeStruct((coarse *...  96 us
    pallas_call x1, Pallas kernels, run_finish(): pl.pallas_call(finish_kernel, out_shape=jax.ShapeDtypeStruct((LEAVES, 1,...  57.9 us
    unnamed x2, local copies, waits for them, and re-layouts  4.44 us

profile of v3, /device:TPU:0, one launch (start us, length us, event | category | flops | bytes accessed | tf_op | source)
XLA Modules:
  0.0 158.3 jit_solution(3145016452623089499)
XLA Ops:
  0.0 1.9 %copy.16.shift_ops = f32[8,121,121]{2,1,0:T(8,128)} copy(f32[8,121,121]{2,0,1:T(8,128)} %param.19) | data formatting | bytes 937024 | tf_op args[5]
  1.9 2.5 %copy.15.m2l_ops = f32[16,121,121]{2,1,0:T(8,128)} copy(f32[16,121,121]{2,0,1:T(8,128)} %param.18) | data formatting | bytes 1874048 | tf_op args[4]
  4.4 96.0 %shard_map.127 = (f32[512,4,512]{2,1,0:T(4,128)}, f32[32,24,128]{2,1,0:T(8,128)}, f32[64,128,512]{2,1,0:T(8,128)}, bf16[64,512,128]{2,1,0:T(8,128)(2,1)}, f32[64...) custom-call(f32[3,32768]{1,0:T(4,128)} %positions.1, f32[64,1,512]{2,1,0:T(1,128)} %bitcast.10, ...), custom_call_target="tpu_custom_call" | custom-call | flops 40000000000 | bytes 60000000 | tf_op jit(solution)/shard_map/pallas_call | solution.py:595
  100.4 57.9 %shard_map.128 = f32[64,1,512]{2,1,0:T(1,128)} custom-call(s32[1,32]{1,0:T(1,128)} %top_list.1, s32[1,32]{1,0:T(1,128)} %top_class.1, s32[8,64]{1,0:T(8,128)} %bitcast.14, s32[8,64]{1,0:T(8,128)} %bitcast.16, s32[32,64]{1,0:T(8,128)} %bitcast.11, s32[32,64]{1,0:T(8,128)} %bitcast.12, f32[16,121,121]{2,1,0:T(8,128)} %copy.15.m2l_ops, ...), custom_call_target="tpu_custom_call" | custom-call | flops 60000002048 | bytes 40000000 | tf_op jit(solution)/shard_map/pallas_call | solution.py:325

commit v4 on v3

--- a/solution.py
+++ b/solution.py
@@ -184,8 +184,11 @@
 
 
 def pad_into(padded, ops):
+    size, classes, width = ops.shape
+    flat = ops.reshape(size * classes, width)
     padded[...] = jnp.zeros_like(padded)
-    padded[:, : ops.shape[1], : ops.shape[2]] = ops[...]
+    for place in range(classes):
+        padded[place, :size, :width] = flat[pl.ds(place, size, stride=classes), :]
 
 
 def local_expansions(pool_moments, m2l, shift, table, far_index, top_class, expansions):
@@ -356,7 +359,7 @@
     in_bodies, in_rows, harmonic_out, left_out, near_out, moments, bodies,
     r1, r2, r3, l1, l2, l3, opposite,
     packs, harmonic, left, near, shift, waves, transposed, column_rows, row_pack,
-    table, tables, table_words, pair_words, pairs,
+    table, tables, table_words, own_table, pair_words, pairs,
     ring_send, ring_recv, small_send, small_recv, plane_send, plane_recv, local_sems, out_sems,
 ):
     gx, gy = lax.axis_index("gx"), lax.axis_index("gy")
@@ -409,20 +412,15 @@
             remote(sources[1], targets[1], ring_send.at[slot + 1], ring_recv.at[slot + 1], back),
         )
 
-    first = ring(1)
     for k in range(1, fine):
         there = lax.rem(gy + k, fine)
         remote(table, tables.at[k], small_send.at[0], small_recv.at[0], {"gy": there})
-    own_table = pltpu.make_async_copy(table, tables.at[0], local_sems.at[0])
-    own_table.start()
-    own_table.wait()
-    others = tables.at[pl.ds(1, fine - 1)]
-    pltpu.make_async_copy(others, others, small_recv.at[0]).wait()
-    words = pltpu.make_async_copy(tables, table_words, local_sems.at[0])
-    words.start()
-    words.wait()
-
-    def pack(block, offset):
+    first = ring(1)
+    own_words = pltpu.make_async_copy(table, own_table, local_sems.at[0])
+    own_words.start()
+    own_words.wait()
+
+    def pack(block, offset, words):
         there = lax.rem(gy + fine - offset, fine)
         buffer = packs.at[offset]
         place = pl.ds((gx * fine + there) * 2, 2)
@@ -431,7 +429,7 @@
             for part in range(4):
                 peer = quad * 4 + part
                 for slot in range(2):
-                    buffer[peer, slot] = block[table_words[offset, slot, peer * fine + gy]]
+                    buffer[peer, slot] = block[words[slot, peer * fine + gy]]
             return carry
 
         lax.fori_loop(0, coarse // 4, one, 0)
@@ -447,7 +445,7 @@
         keep.start()
         return keep
 
-    kept = [pack(bodies, 0)]
+    kept = [pack(bodies, 0, own_table)]
 
     word, taken, _, _ = near_fields(near_src, near_shift)
     pair_words[...] = jnp.zeros_like(pair_words)
@@ -494,20 +492,20 @@
         return carry
 
     left[...] = jnp.zeros_like(left)
-    cuts = (0, 24, 48, 64)
-    lax.fori_loop(cuts[0] // 4, cuts[1] // 4, feature_step, 0)
+    lax.fori_loop(0, half // 4, feature_step, 0)
 
     first[0].wait_recv()
     first[1].wait_recv()
     second = ring(2)
-    kept += [pack(r1, 1), pack(l1, fine - 1)]
-    lax.fori_loop(cuts[1] // 4, cuts[2] // 4, feature_step, 0)
-
-    second[0].wait_recv()
-    second[1].wait_recv()
-    third = ring(3)
-    kept += [pack(r2, 2), pack(l2, fine - 2)]
-    lax.fori_loop(cuts[2] // 4, cuts[3] // 4, feature_step, 0)
+    sent_tables = tables.at[pl.ds(1, fine - 1)]
+    pltpu.make_async_copy(sent_tables, sent_tables, small_recv.at[0]).wait()
+    words = pltpu.make_async_copy(
+        sent_tables, table_words.at[pl.ds(1, fine - 1)], local_sems.at[0]
+    )
+    words.start()
+    words.wait()
+    kept += [pack(r1, 1, table_words.at[1]), pack(l1, fine - 1, table_words.at[fine - 1])]
+    lax.fori_loop(half // 4, LEAVES // 4, feature_step, 0)
 
     outs = [
         pltpu.make_async_copy(harmonic, harmonic_out, out_sems.at[0]),
@@ -523,19 +521,20 @@
         remote(column_rows.at[0], column_rows.at[k], small_send.at[1], small_recv.at[1],
                {"gy": lax.rem(gy + k, fine)})
 
+    second[0].wait_recv()
+    second[1].wait_recv()
+    third = ring(3)
+    kept += [pack(r2, 2, table_words.at[2]), pack(l2, fine - 2, table_words.at[fine - 2])]
+    lax.fori_loop(0, half // 4, near_step, 0)
+    outs.append(
+        pltpu.make_async_copy(near.at[pl.ds(0, half)], near_out.at[pl.ds(0, half)], out_sems.at[2])
+    )
+    outs[-1].start()
+
     third[0].wait_recv()
     third[1].wait_recv()
     fourth = ring(4)
-    kept += [pack(r3, 3), pack(l3, fine - 3)]
-    lax.fori_loop(0, half // 4, near_step, 0)
-    outs.append(
-        pltpu.make_async_copy(near.at[pl.ds(0, half)], near_out.at[pl.ds(0, half)], out_sems.at[2])
-    )
-    outs[-1].start()
-
-    fourth[0].wait_recv()
-    fourth[1].wait_recv()
-    kept += [pack(opposite, fine // 2)]
+    kept += [pack(r3, 3, table_words.at[3]), pack(l3, fine - 3, table_words.at[fine - 3])]
 
     others = column_rows.at[pl.ds(1, fine - 1)]
     pltpu.make_async_copy(others, others, small_recv.at[1]).wait()
@@ -546,7 +545,9 @@
             for part in range(4):
                 peer = quad * 4 + part
                 for slot in range(2):
-                    row = table_words[offset, slot, peer * fine + gy]
+                    row = (table_words.at[offset] if offset else own_table)[
+                        slot, peer * fine + gy
+                    ]
                     row_pack[peer, pl.ds(there * 2 + slot, 1), :] = column_rows[
                         offset, pl.ds(row, 1), :
                     ]
@@ -567,6 +568,10 @@
     keep.start()
     kept.append(keep)
 
+    fourth[0].wait_recv()
+    fourth[1].wait_recv()
+    kept += [pack(opposite, fine // 2, table_words.at[fine // 2])]
+
     lax.fori_loop(half // 4, LEAVES // 4, near_step, 0)
     outs.append(
         pltpu.make_async_copy(
@@ -579,7 +584,6 @@
         copy.wait()
     for copy in first + second + third + fourth:
         copy.wait_send()
-    sent_tables = tables.at[pl.ds(1, fine - 1)]
     pltpu.make_async_copy(sent_tables, sent_tables, small_send.at[0]).wait()
     pltpu.make_async_copy(others, others, small_send.at[1]).wait()
     sent = in_bodies.at[pl.ds(0, (coarse - 1) * fine * 2)]
@@ -619,6 +623,7 @@
             pltpu.VMEM((8, coarse * fine), jnp.int32),
             pltpu.VMEM((fine, 8, coarse * fine), jnp.int32),
             pltpu.SMEM((fine, 8, coarse * fine), jnp.int32),
+            pltpu.SMEM((8, coarse * fine), jnp.int32),
             pltpu.VMEM((8, 128), jnp.int32),
             pltpu.SMEM((8, 128), jnp.int32),
             pltpu.SemaphoreType.DMA((8,)),
@@ -662,13 +667,13 @@
         near_shift.T,
         moment_freq,
         moment_phase[None],
-        child_parent_shift_matrix,
+        child_parent_shift_matrix.transpose(1, 0, 2),
         lax.axis_size("gx"),
         lax.axis_size("gy"),
     )
     result = run_finish(
         top_list, top_class, near_src.T, near_shift.T, far_src.T, far_class.T,
-        m2l_ops, child_parent_shift_matrix, moments, in_rows,
+        m2l_ops.transpose(1, 0, 2), child_parent_shift_matrix.transpose(1, 0, 2), moments, in_rows,
         left, near, harmonic, bodies, in_bodies,
     )
     return result.reshape(leaves * WIDTH)

time: 159 us -> 136 us (0.86)
  the two profiles are of different devices: /device:TPU:0 before, /device:TPU:6 now
where the time goes in v4:
time: 136 us; the launch traced here: 135 us
  Pallas kernels  135 us (99%)
    pallas_call x1, Pallas kernels, run_exchange(): pl.pallas_call(exchange_kernel, out_shape=[jax.ShapeDtypeStruct((coarse *...  80 us
    pallas_call x1, Pallas kernels, run_finish(): pl.pallas_call(finish_kernel, out_shape=jax.ShapeDtypeStruct((LEAVES, 1,...  55.3 us

profile of v4, /device:TPU:6, one launch (start us, length us, event | category | flops | bytes accessed | tf_op | source)
XLA Modules:
  0.0 135.3 jit_solution(2778471753534659558)
XLA Ops:
  0.0 80.0 %shard_map.127 = (f32[512,4,512]{2,1,0:T(4,128)}, f32[32,24,128]{2,1,0:T(8,128)}, f32[64,128,512]{2,1,0:T(8,128)}, bf16[64,512,128]{2,1,0:T(8,128)(2,1)}, f32[64...) custom-call(f32[3,32768]{1,0:T(4,128)} %positions.1, f32[64,1,512]{2,1,0:T(1,128)} %bitcast.15, ...), custom_call_target="tpu_custom_call" | custom-call | flops 40000000000 | bytes 60000000 | tf_op jit(solution)/shard_map/pallas_call | solution.py:599
  80.0 55.3 %shard_map.128 = f32[64,1,512]{2,1,0:T(1,128)} custom-call(s32[1,32]{1,0:T(1,128)} %top_list.1, s32[1,32]{1,0:T(1,128)} %top_class.1, s32[8,64]{1,0:T(8,128)} %bitcast.19, s32[8,64]{1,0:T(8,128)} %bitcast.21, s32[32,64]{1,0:T(8,128)} %bitcast.16, s32[32,64]{1,0:T(8,128)} %bitcast.17, f32[121,16,121]{2,1,0:T(8,128)} %bitcast.12, f32[121,8,121]{2,1,0:T(8,128)} %bitcast.14, ...), custom_call_target="tpu_custom_call" | custom-call | flops 60000002048 | bytes 40000000 | tf_op jit(solution)/shard_map/pallas_call | solution.py:328

commit v5 on v4

--- a/solution.py
+++ b/solution.py
@@ -159,28 +159,36 @@
 
 def near_list(near_src, near_shift, listed):
     word, _, wanted, source = near_fields(near_src, near_shift)
-    word = word + (source * 63 + lax.broadcasted_iota(jnp.int32, source.shape, 1)).astype(F32)
+    lane = lax.broadcasted_iota(jnp.int32, source.shape, 1)
+    slot = source - LEAVES
+    back = (lax.axis_index("gy") - (slot >> 1)) & 7
+    position = jnp.where(
+        back == 0, 0, jnp.where(back < 4, 2 * back - 1, jnp.where(back == 4, 7, 16 - 2 * back))
+    )
+    place = jnp.where(slot < 0, source, LEAVES + (slot >> 4) * 16 + position * 2 + (slot & 1))
+    word = word + (place * 64 - source + lane).astype(F32)
     mark = jnp.where(wanted, 1.0, 0.0)
-    before = lax.broadcasted_iota(jnp.int32, (LEAVES, LEAVES), 0)
-    before = before < lax.broadcasted_iota(jnp.int32, (LEAVES, LEAVES), 1)
-    place = dot_nn(mark.astype(BF16), jnp.where(before, 1.0, 0.0).astype(BF16))
-    totals = jnp.sum(mark, axis=1, keepdims=True)
+    first = lax.broadcasted_iota(jnp.int32, (LEAVES, LEAVES), 0)
+    second = lax.broadcasted_iota(jnp.int32, (LEAVES, LEAVES), 1)
+    same = (first >> 5) == (second >> 5)
+    before = jnp.where(same & (first < second), 1.0, 0.0).astype(BF16)
+    rank = dot_nn(mark.astype(BF16), before)
+    totals = dot_nn(mark.astype(BF16), jnp.where(same, 1.0, 0.0).astype(BF16))
     row = lax.broadcasted_iota(jnp.int32, (8, LEAVES), 0)
     for column in range(8):
-        place = place + jnp.where(row > column, totals[column : column + 1], 0.0)
-    place = jnp.where(wanted, place, -1.0).astype(jnp.int32)
+        rank = rank + jnp.where(row > column, totals[column : column + 1], 0.0)
+    rank = rank.astype(jnp.int32) + (lane >> 5) * 256
+    rank = jnp.where(wanted, rank, -1)
     parts = split3(word)
-    low_row = lax.broadcasted_iota(jnp.int32, (LEAVES, LEAVES), 0)
     codes = jnp.zeros((8, LEAVES), F32)
     for column in range(8):
-        at = place[column : column + 1]
-        low = jnp.where(low_row == (at & 63), 1.0, 0.0).astype(BF16)
+        at = rank[column : column + 1]
+        low = jnp.where(first == (at & 63), 1.0, 0.0).astype(BF16)
         for part in parts:
             high = jnp.where(row == (at >> 6), part[column : column + 1], 0.0).astype(BF16)
             codes = codes + dot_nt(high, low)
-    number = jnp.broadcast_to(jnp.sum(totals, axis=0, keepdims=True), (8, 128))
-    listed[...] = number.astype(jnp.int32)
-    listed[:, :LEAVES] = codes.astype(jnp.int32)
+    number = jnp.broadcast_to(jnp.sum(totals, axis=0, keepdims=True), (8, LEAVES))
+    listed[...] = jnp.concatenate([codes, number], axis=1).astype(jnp.int32)
 
 
 def pad_into(padded, ops):
@@ -241,7 +249,11 @@
                 (left_hbm, left),
                 (bodies_hbm, pool.at[pl.ds(0, LEAVES)]),
                 (in_bodies_hbm, pool.at[pl.ds(LEAVES, slots)]),
-                (near_hbm, near),
+                (near_hbm.at[pl.ds(0, LEAVES // 2)], near.at[pl.ds(0, LEAVES // 2)]),
+                (
+                    near_hbm.at[pl.ds(LEAVES // 2, LEAVES // 2)],
+                    near.at[pl.ds(LEAVES // 2, LEAVES // 2)],
+                ),
                 (harmonic_hbm, harmonic),
             )
         )
@@ -256,8 +268,8 @@
     )
     near_list(near_src, near_shift, listed)
     words = [
-        pltpu.make_async_copy(far_rows, far_index, sems.at[5]),
-        pltpu.make_async_copy(listed, codes, sems.at[6]),
+        pltpu.make_async_copy(far_rows, far_index, sems.at[6]),
+        pltpu.make_async_copy(listed, codes, sems.at[7]),
     ]
     for copy in words:
         copy.start()
@@ -282,9 +294,9 @@
     for copy in copies[:4]:
         copy.wait()
 
-    def near_step(group, carry):
+    def near_step(group, half):
         for member in range(UNROLL):
-            code = codes[group >> 3, (group & 7) * UNROLL + member]
+            code = codes[4 * half + (group >> 3), (group & 7) * UNROLL + member]
             target = code & 63
             source = (code >> 6) & 1023
             live = (code >> 21).astype(F32)
@@ -295,10 +307,12 @@
                 near[target, start : start + 128] += pair_rows(
                     left.at[target][:, :GROUPS], right, charge, start, 128
                 )
-        return carry
+        return half
 
     lax.fori_loop(0, (codes[0, LEAVES] + UNROLL - 1) // UNROLL, near_step, 0)
     copies[4].wait()
+    lax.fori_loop(0, (codes[0, LEAVES + 32] + UNROLL - 1) // UNROLL, near_step, 1)
+    copies[5].wait()
     ones = jnp.ones((8, 128), BF16)
 
     def far_step(group, columns):
@@ -344,7 +358,7 @@
             pltpu.VMEM((32, 128), jnp.int32),
             pltpu.SMEM((8, 128), jnp.int32),
             pltpu.SMEM((32, 128), jnp.int32),
-            pltpu.SemaphoreType.DMA((7,)),
+            pltpu.SemaphoreType.DMA((8,)),
         ],
         compiler_params=pltpu.CompilerParams(vmem_limit_bytes=62 << 20),
         cost_estimate=pl.CostEstimate(flops=60_000_000_000, bytes_accessed=40_000_000, transcendentals=0),
@@ -358,7 +372,7 @@
     positions, charges, send_table, near_src, near_shift, freq, phase, shift_ops,
     in_bodies, in_rows, harmonic_out, left_out, near_out, moments, bodies,
     r1, r2, r3, l1, l2, l3, opposite,
-    packs, harmonic, left, near, shift, waves, transposed, column_rows, row_pack,
+    singles, doubles, harmonic, left, near, shift, waves, transposed, column_rows, top_rows, row_pack,
     table, tables, table_words, own_table, pair_words, pairs,
     ring_send, ring_recv, small_send, small_recv, plane_send, plane_recv, local_sems, out_sems,
 ):
@@ -420,16 +434,16 @@
     own_words.start()
     own_words.wait()
 
-    def pack(block, offset, words):
-        there = lax.rem(gy + fine - offset, fine)
-        buffer = packs.at[offset]
-        place = pl.ds((gx * fine + there) * 2, 2)
+    def pack(buffer, position, sources):
+        records = 2 * len(sources)
+        place = pl.ds((gx * fine + position) * 2, records)
 
         def one(quad, carry):
             for part in range(4):
                 peer = quad * 4 + part
-                for slot in range(2):
-                    buffer[peer, slot] = block[words[slot, peer * fine + gy]]
+                for number, (block, words) in enumerate(sources):
+                    for slot in range(2):
+                        buffer[peer, 2 * number + slot] = block[words[slot, peer * fine + gy]]
             return carry
 
         lax.fori_loop(0, coarse // 4, one, 0)
@@ -441,11 +455,11 @@
             return carry
 
         lax.fori_loop(1, coarse, push, 0)
-        keep = pltpu.make_async_copy(buffer.at[gx], in_bodies.at[place], local_sems.at[1 + offset])
+        keep = pltpu.make_async_copy(buffer.at[gx], in_bodies.at[place], local_sems.at[1 + position])
         keep.start()
         return keep
 
-    kept = [pack(bodies, 0, own_table)]
+    kept = [pack(singles.at[0], 0, [(bodies, own_table)])]
 
     word, taken, _, _ = near_fields(near_src, near_shift)
     pair_words[...] = jnp.zeros_like(pair_words)
@@ -464,9 +478,9 @@
     lane = lax.broadcasted_iota(jnp.int32, (KPAD, KPAD), 1)
     transposed[...] = jnp.zeros_like(transposed)
 
-    def feature_step(quad, carry):
-        for member in range(4):
-            leaf = quad * 4 + member
+    def feature_step(eight, carry):
+        for member in range(8):
+            leaf = eight * 8 + member
             body = pad8(bodies[leaf])
             basis = basis_leaf(body, weights)
             harmonic[leaf] = basis
@@ -492,7 +506,7 @@
         return carry
 
     left[...] = jnp.zeros_like(left)
-    lax.fori_loop(0, half // 4, feature_step, 0)
+    lax.fori_loop(0, half // 8, feature_step, 0)
 
     first[0].wait_recv()
     first[1].wait_recv()
@@ -504,8 +518,10 @@
     )
     words.start()
     words.wait()
-    kept += [pack(r1, 1, table_words.at[1]), pack(l1, fine - 1, table_words.at[fine - 1])]
-    lax.fori_loop(half // 4, LEAVES // 4, feature_step, 0)
+    kept.append(
+        pack(doubles.at[0], 1, [(r1, table_words.at[1]), (l1, table_words.at[fine - 1])])
+    )
+    lax.fori_loop(half // 8, LEAVES // 8, feature_step, 0)
 
     outs = [
         pltpu.make_async_copy(harmonic, harmonic_out, out_sems.at[0]),
@@ -524,7 +540,9 @@
     second[0].wait_recv()
     second[1].wait_recv()
     third = ring(3)
-    kept += [pack(r2, 2, table_words.at[2]), pack(l2, fine - 2, table_words.at[fine - 2])]
+    kept.append(
+        pack(doubles.at[1], 3, [(r2, table_words.at[2]), (l2, table_words.at[fine - 2])])
+    )
     lax.fori_loop(0, half // 4, near_step, 0)
     outs.append(
         pltpu.make_async_copy(near.at[pl.ds(0, half)], near_out.at[pl.ds(0, half)], out_sems.at[2])
@@ -534,7 +552,9 @@
     third[0].wait_recv()
     third[1].wait_recv()
     fourth = ring(4)
-    kept += [pack(r3, 3, table_words.at[3]), pack(l3, fine - 3, table_words.at[fine - 3])]
+    kept.append(
+        pack(doubles.at[2], 5, [(r3, table_words.at[3]), (l3, table_words.at[fine - 3])])
+    )
 
     others = column_rows.at[pl.ds(1, fine - 1)]
     pltpu.make_async_copy(others, others, small_recv.at[1]).wait()
@@ -551,12 +571,14 @@
                     row_pack[peer, pl.ds(there * 2 + slot, 1), :] = column_rows[
                         offset, pl.ds(row, 1), :
                     ]
-                row_pack[peer, pl.ds(2 * fine + there, 1), :] = column_rows[
-                    offset, LEAVES : LEAVES + 1, :
-                ]
             return carry
 
         lax.fori_loop(0, coarse // 4, pick, 0)
+        top_rows[pl.ds(there, 1), :] = column_rows[offset, LEAVES : LEAVES + 1, :]
+
+    all_tops = top_rows[...]
+    for peer in range(coarse):
+        row_pack[peer, 2 * fine :] = all_tops
 
     def push_rows(j, carry):
         peer = lax.rem(gx + j, coarse)
@@ -570,7 +592,7 @@
 
     fourth[0].wait_recv()
     fourth[1].wait_recv()
-    kept += [pack(opposite, fine // 2, table_words.at[fine // 2])]
+    kept.append(pack(singles.at[1], fine - 1, [(opposite, table_words.at[fine // 2])]))
 
     lax.fori_loop(half // 4, LEAVES // 4, near_step, 0)
     outs.append(
@@ -611,7 +633,8 @@
         out_specs=[ANY] * 5 + [VMEM] * 2,
         scratch_shapes=[block] * 7
         + [
-            pltpu.VMEM((fine, coarse, 2, 4, WIDTH), F32),
+            pltpu.VMEM((2, coarse, 2, 4, WIDTH), F32),
+            pltpu.VMEM((3, coarse, 4, 4, WIDTH), F32),
             pltpu.VMEM((LEAVES, KPAD, WIDTH), F32),
             pltpu.VMEM((LEAVES, WIDTH, 128), BF16),
             pltpu.VMEM((LEAVES, WIDTH, 128), F32),
@@ -619,6 +642,7 @@
             pltpu.VMEM((4, KPAD), F32),
             pltpu.VMEM((KPAD, KPAD), F32),
             pltpu.VMEM((fine, LEAVES + 8, KPAD), F32),
+            pltpu.VMEM((fine, KPAD), F32),
             pltpu.VMEM((coarse, 3 * fine, KPAD), F32),
             pltpu.VMEM((8, coarse * fine), jnp.int32),
             pltpu.VMEM((fine, 8, coarse * fine), jnp.int32),

time: 136 us -> 137 us (level)
  the two profiles are of different devices: /device:TPU:6 before, /device:TPU:1 now
where the time goes in v5:
time: 137 us; the launch traced here: 135 us
  Pallas kernels  135 us (99%)
    pallas_call x1, Pallas kernels, run_exchange(): pl.pallas_call(exchange_kernel, out_shape=[jax.ShapeDtypeStruct((coarse *...  82.5 us
    pallas_call x1, Pallas kernels, run_finish(): pl.pallas_call(finish_kernel, out_shape=jax.ShapeDtypeStruct((LEAVES, 1,...  52.1 us

profile of v5, /device:TPU:1, one launch (start us, length us, event | category | flops | bytes accessed | tf_op | source)
XLA Modules:
  0.0 134.8 jit_solution(13883524524809293289)
XLA Ops:
  0.0 82.5 %shard_map.127 = (f32[512,4,512]{2,1,0:T(4,128)}, f32[32,24,128]{2,1,0:T(8,128)}, f32[64,128,512]{2,1,0:T(8,128)}, bf16[64,512,128]{2,1,0:T(8,128)(2,1)}, f32[64...) custom-call(f32[3,32768]{1,0:T(4,128)} %positions.1, f32[64,1,512]{2,1,0:T(1,128)} %bitcast.15, ...), custom_call_target="tpu_custom_call" | custom-call | flops 40000000000 | bytes 60000000 | tf_op jit(solution)/shard_map/pallas_call | solution.py:621
  82.6 52.1 %shard_map.128 = f32[64,1,512]{2,1,0:T(1,128)} custom-call(s32[1,32]{1,0:T(1,128)} %top_list.1, s32[1,32]{1,0:T(1,128)} %top_class.1, s32[8,64]{1,0:T(8,128)} %bitcast.19, s32[8,64]{1,0:T(8,128)} %bitcast.21, s32[32,64]{1,0:T(8,128)} %bitcast.16, s32[32,64]{1,0:T(8,128)} %bitcast.17, f32[121,16,121]{2,1,0:T(8,128)} %bitcast.12, f32[121,8,121]{2,1,0:T(8,128)} %bitcast.14, ...), custom_call_target="tpu_custom_call" | custom-call | flops 60000002048 | bytes 40000000 | tf_op jit(solution)/shard_map/pallas_call | solution.py:342

commit v6 on v5

--- a/solution.py
+++ b/solution.py
@@ -505,6 +505,11 @@
                 )
         return carry
 
+    def near_away(start, stop, place):
+        rows = pl.ds(start, stop - start)
+        outs.append(pltpu.make_async_copy(near.at[rows], near_out.at[rows], out_sems.at[place]))
+        outs[-1].start()
+
     left[...] = jnp.zeros_like(left)
     lax.fori_loop(0, half // 8, feature_step, 0)
 
@@ -521,7 +526,15 @@
     kept.append(
         pack(doubles.at[0], 1, [(r1, table_words.at[1]), (l1, table_words.at[fine - 1])])
     )
-    lax.fori_loop(half // 8, LEAVES // 8, feature_step, 0)
+    lax.fori_loop(half // 8, LEAVES // 8 - 1, feature_step, 0)
+
+    second[0].wait_recv()
+    second[1].wait_recv()
+    third = ring(3)
+    kept.append(
+        pack(doubles.at[1], 3, [(r2, table_words.at[2]), (l2, table_words.at[fine - 2])])
+    )
+    lax.fori_loop(LEAVES // 8 - 1, LEAVES // 8, feature_step, 0)
 
     outs = [
         pltpu.make_async_copy(harmonic, harmonic_out, out_sems.at[0]),
@@ -537,17 +550,7 @@
         remote(column_rows.at[0], column_rows.at[k], small_send.at[1], small_recv.at[1],
                {"gy": lax.rem(gy + k, fine)})
 
-    second[0].wait_recv()
-    second[1].wait_recv()
-    third = ring(3)
-    kept.append(
-        pack(doubles.at[1], 3, [(r2, table_words.at[2]), (l2, table_words.at[fine - 2])])
-    )
-    lax.fori_loop(0, half // 4, near_step, 0)
-    outs.append(
-        pltpu.make_async_copy(near.at[pl.ds(0, half)], near_out.at[pl.ds(0, half)], out_sems.at[2])
-    )
-    outs[-1].start()
+    lax.fori_loop(0, 4, near_step, 0)
 
     third[0].wait_recv()
     third[1].wait_recv()
@@ -555,6 +558,13 @@
     kept.append(
         pack(doubles.at[2], 5, [(r3, table_words.at[3]), (l3, table_words.at[fine - 3])])
     )
+
+    lax.fori_loop(4, 6, near_step, 0)
+    near_away(0, 24, 2)
+
+    fourth[0].wait_recv()
+    fourth[1].wait_recv()
+    kept.append(pack(singles.at[1], fine - 1, [(opposite, table_words.at[fine // 2])]))
 
     others = column_rows.at[pl.ds(1, fine - 1)]
     pltpu.make_async_copy(others, others, small_recv.at[1]).wait()
@@ -590,17 +600,10 @@
     keep.start()
     kept.append(keep)
 
-    fourth[0].wait_recv()
-    fourth[1].wait_recv()
-    kept.append(pack(singles.at[1], fine - 1, [(opposite, table_words.at[fine // 2])]))
-
-    lax.fori_loop(half // 4, LEAVES // 4, near_step, 0)
-    outs.append(
-        pltpu.make_async_copy(
-            near.at[pl.ds(half, half)], near_out.at[pl.ds(half, half)], out_sems.at[3]
-        )
-    )
-    outs[-1].start()
+    lax.fori_loop(6, 11, near_step, 0)
+    near_away(24, 44, 3)
+    lax.fori_loop(11, LEAVES // 4, near_step, 0)
+    near_away(44, LEAVES, 4)
 
     for copy in kept + outs:
         copy.wait()
@@ -657,7 +660,7 @@
             pltpu.SemaphoreType.DMA((2,)),
             pltpu.SemaphoreType.DMA((2,)),
             pltpu.SemaphoreType.DMA((1 + fine,)),
-            pltpu.SemaphoreType.DMA((4,)),
+            pltpu.SemaphoreType.DMA((5,)),
         ],
         compiler_params=pltpu.CompilerParams(
             vmem_limit_bytes=62 << 20, collective_id=0, has_side_effects=True

time: 137 us -> 139 us (1.015)
  the two profiles are of different devices: /device:TPU:1 before, /device:TPU:6 now
where the time goes in v6:
time: 139 us; the launch traced here: 138 us
  Pallas kernels  138 us (99%)
    pallas_call x1, Pallas kernels, run_exchange(): pl.pallas_call(exchange_kernel, out_shape=[jax.ShapeDtypeStruct((coarse *...  82.1 us
    pallas_call x1, Pallas kernels, run_finish(): pl.pallas_call(finish_kernel, out_shape=jax.ShapeDtypeStruct((LEAVES, 1,...  55.7 us

profile of v6, /device:TPU:6, one launch (start us, length us, event | category | flops | bytes accessed | tf_op | source)
XLA Modules:
  0.0 138.0 jit_solution(5876135161150025067)
XLA Ops:
  0.0 82.1 %shard_map.127 = (f32[512,4,512]{2,1,0:T(4,128)}, f32[32,24,128]{2,1,0:T(8,128)}, f32[64,128,512]{2,1,0:T(8,128)}, bf16[64,512,128]{2,1,0:T(8,128)(2,1)}, f32[64...) custom-call(f32[3,32768]{1,0:T(4,128)} %positions.1, f32[64,1,512]{2,1,0:T(1,128)} %bitcast.15, ...), custom_call_target="tpu_custom_call" | custom-call | flops 40000000000 | bytes 60000000 | tf_op jit(solution)/shard_map/pallas_call | solution.py:624
  82.1 55.7 %shard_map.128 = f32[64,1,512]{2,1,0:T(1,128)} custom-call(s32[1,32]{1,0:T(1,128)} %top_list.1, s32[1,32]{1,0:T(1,128)} %top_class.1, s32[8,64]{1,0:T(8,128)} %bitcast.19, s32[8,64]{1,0:T(8,128)} %bitcast.21, s32[32,64]{1,0:T(8,128)} %bitcast.16, s32[32,64]{1,0:T(8,128)} %bitcast.17, f32[121,16,121]{2,1,0:T(8,128)} %bitcast.12, f32[121,8,121]{2,1,0:T(8,128)} %bitcast.14, ...), custom_call_target="tpu_custom_call" | custom-call | flops 60000002048 | bytes 40000000 | tf_op jit(solution)/shard_map/pallas_call | solution.py:342
